TPU v7x, 32 devices: a whole 2x2x4 slice. The times are simulated.
32 devices in a mesh: tm: 16 (over z, x, core), head: 2 (over y).
Axes of the slice: x: 2, y: 2, z: 4, core: 2. Of those that a mesh axis runs over, the one named last changes fastest.
Arguments:
- frames: bfloat16 [4096, 1280], P('tm', 'head'), may hold values from -6 to 6
- segment_ids: int32 [4096], replicated, may hold values from 0 to 31, never falling along the last dimension, each value on 1 to 256 neighbouring positions
- ln_gain: float32 [1280], replicated, may hold values from 0.5 to 1.5
- ln_bias: float32 [1280], replicated, may hold values from -1.5 to 1.5
- qkv_weight: bfloat16 [3, 1280, 1024], P(None, None, 'head'), may hold values from -3 to 3
- out_weight: bfloat16 [1024, 1280], P(None, 'head'), may hold values from -0.1875 to 0.1875
- out_bias: float32 [1280], P('head'), may hold values from -2.5 to 2.5
- adapter: bfloat16 [1280, 2560], P('head'), may hold values from -0.15625 to 0.15625
- rms_gain: float32 [2560], replicated, may hold values from 0.25 to 1.75
- x_weight: bfloat16 [2560, 2560], P(None, 'head'), may hold values from -0.125 to 0.125
- bc_weight: bfloat16 [2560, 256], P(None, 'head'), may hold values from -0.125 to 0.125
- decay: float32 [1024, 40], P('tm', 'head'), may hold values from 0 to 1
- skip_gain: float32 [40], P('head'), may hold values from 0.5 to 1.5
Outputs:
- encoded: bfloat16 [4096, 1280], P('tm', 'head')
- mixed: bfloat16 [1024, 2560], P('tm', 'head')
Inputs may be any that keep to these rules, and one draw needn't show every extreme that they name: `segment_ids`: segment numbers never fall along the frames; each segment holds 1 to 256 frames and one holds exactly 256.
All inputs are finite; a program needn't handle non-finite values.
Results may differ from a plain program's by a relative error of at most 0.008.
Values may be sent and summed in bfloat16 or wider, within the bound.
A program may use at most 64 MiB of HBM per device.

v0:
```python
import math

import jax
import jax.numpy as jnp
from jax import lax
from jax.sharding import PartitionSpec as P

EHEAD_DIM = 64
HDIM = 64
NSTATE = 128
WINDOW = 256


EPSILON = 1e-05
HIGHEST = lax.Precision.HIGHEST


def with_halo(block, sides, width):
    for axis, dim in sides:
        count = lax.axis_size(axis)
        forward = [(i, i + 1) for i in range(count - 1)]
        backward = [(target, source) for source, target in forward]
        low = lax.ppermute(
            lax.slice_in_dim(block, block.shape[dim] - width, None, axis=dim), axis, forward
        )
        high = lax.ppermute(lax.slice_in_dim(block, 0, width, axis=dim), axis, backward)
        block = jnp.concatenate([low, block, high], axis=dim)
    return block


def prefix(part, axis, combine, identity):
    place = lax.axis_index(axis)
    gathered = jax.tree.map(lambda a: lax.all_gather(a, axis), part)
    state = jax.tree.map(lambda a, e: jnp.zeros_like(a) + jnp.asarray(e, a.dtype), part, identity)

    def one(hop, state):
        return combine(
            state, jax.tree.map(lambda a: lax.dynamic_index_in_dim(a, hop, 0, False), gathered)
        )

    return lax.fori_loop(0, place, one, state)


def layer_norm(values, gain, offset):
    center_mean = jnp.mean(values, axis=-1, keepdims=True)
    spread = jnp.mean(jnp.square(values - center_mean), axis=-1, keepdims=True)
    return (values - center_mean) * lax.rsqrt(spread + EPSILON) * gain + offset


def block_terms(inputs, b_in, c_in, decay):
    log_decay = jnp.log(decay)
    cumulative = jnp.cumsum(log_decay, axis=0)
    length = inputs.shape[0]
    sequence_indices = jnp.arange(length, dtype=jnp.int32)
    causal = sequence_indices[:, None] >= sequence_indices[None, :]
    log_gap = cumulative[:, None, :] - cumulative[None, :, :]
    weights = jnp.exp(jnp.where(causal[:, :, None], log_gap, -1e30))
    driven = inputs * (1.0 - decay)[:, :, None]
    affinity = jnp.dot(c_in, b_in.T, preferred_element_type=jnp.float32)
    within = jnp.einsum("tsh,shp->thp", affinity[:, :, None] * weights, driven, precision=HIGHEST)
    tail_decay = jnp.exp(cumulative[-1][None, :] - cumulative)
    end_state = jnp.einsum(
        "sh,shp,sn->hpn", tail_decay, driven, b_in.astype(jnp.float32), precision=HIGHEST
    )
    return (within, jnp.exp(cumulative), jnp.exp(cumulative[-1]), end_state)


def combine_states(earlier, later):
    return (earlier[0] * later[0], later[0][:, None, None] * earlier[1] + later[1])


def per_device(
    frames,
    segment_ids,
    ln_gain,
    ln_bias,
    qkv_weight,
    out_weight,
    out_bias,
    adapter,
    rms_gain,
    x_weight,
    bc_weight,
    decay,
    skip_gain,
):
    frame_count = frames.shape[0]
    margin = WINDOW
    tm_slot = lax.axis_index("tm")
    adapter_cols = lax.all_to_all(adapter, "head", split_axis=1, concat_axis=0, tiled=True)
    gathered = lax.all_gather(frames, "head", axis=1, tiled=True)
    normed = layer_norm(gathered.astype(jnp.float32), ln_gain, ln_bias).astype(jnp.bfloat16)
    queries = jnp.dot(normed, qkv_weight[0], preferred_element_type=jnp.float32).astype(
        jnp.bfloat16
    )
    keys_own = jnp.dot(normed, qkv_weight[1], preferred_element_type=jnp.float32).astype(
        jnp.bfloat16
    )
    values_own = jnp.dot(normed, qkv_weight[2], preferred_element_type=jnp.float32).astype(
        jnp.bfloat16
    )
    joined = jnp.concatenate([keys_own, values_own], axis=1)
    extended = with_halo(joined, (("tm", 0),), margin)
    head_width = keys_own.shape[1]
    keys_ext = extended[:, :head_width]
    values_ext = extended[:, head_width:]
    ids_pad = jnp.pad(segment_ids, (margin, margin), constant_values=-1)
    local_ids = lax.dynamic_slice_in_dim(
        ids_pad, tm_slot * frame_count, frame_count + 2 * margin, 0
    )
    heads_dev = queries.shape[1] // EHEAD_DIM
    qblock = math.gcd(frame_count, 512)
    span_rows = qblock + 2 * margin

    def attend(block_index):
        begin = block_index * qblock
        query_rows = queries.reshape(qblock, heads_dev, EHEAD_DIM)
        key_rows = keys_ext.reshape(span_rows, heads_dev, EHEAD_DIM)
        value_rows = values_ext.reshape(span_rows, heads_dev, EHEAD_DIM)
        query_ids = lax.dynamic_slice_in_dim(local_ids, begin + margin, qblock, 0)
        scores = jnp.einsum(
            "qhe,khe->hqk", query_rows, key_rows, preferred_element_type=jnp.float32
        ) * EHEAD_DIM ** (-0.5)
        allowed = query_ids[:, None] == local_ids[None, :]
        scores = jnp.where(allowed[None], scores, -1e30)
        peak = jnp.max(scores, axis=-1, keepdims=True)
        raised = jnp.exp(scores - peak)
        probs = (raised / jnp.sum(raised, axis=-1, keepdims=True)).astype(jnp.bfloat16)
        blended = jnp.einsum("hqk,khe->qhe", probs, value_rows, preferred_element_type=jnp.float32)
        return blended.astype(jnp.bfloat16).reshape(qblock, heads_dev * EHEAD_DIM)

    attended = lax.map(attend, jnp.arange(frame_count // qblock, dtype=jnp.int32)).reshape(
        frame_count, heads_dev * EHEAD_DIM
    )
    attention = jnp.dot(
        lax.all_gather(attended, "head", axis=1, tiled=True),
        out_weight,
        preferred_element_type=jnp.float32,
    )
    encoded = (frames.astype(jnp.float32) + attention + out_bias).astype(jnp.bfloat16)
    pooled = jnp.mean(
        encoded.astype(jnp.float32).reshape(frame_count // 4, 4, encoded.shape[1]), axis=1
    ).astype(jnp.bfloat16)
    pooled_all = lax.all_gather(pooled, "head", axis=1, tiled=True)
    column_part = jnp.dot(pooled_all, adapter_cols, preferred_element_type=jnp.float32)
    column_width = column_part.shape[1]
    column_sq = lax.psum(jnp.sum(jnp.square(column_part), axis=1), "head")
    column_gain = lax.dynamic_slice_in_dim(
        rms_gain, lax.axis_index("head") * column_width, column_width, 0
    )
    column_scaled = (
        column_part * lax.rsqrt(column_sq[:, None] / rms_gain.shape[0] + EPSILON) * column_gain
    ).astype(jnp.bfloat16)
    scaled = lax.all_gather(column_scaled, "head", axis=1, tiled=True)
    inputs = jax.nn.silu(jnp.dot(scaled, x_weight, preferred_element_type=jnp.float32)).astype(
        jnp.bfloat16
    )
    coupler_part = jax.nn.silu(
        jnp.dot(scaled, bc_weight, preferred_element_type=jnp.float32)
    ).astype(jnp.bfloat16)
    couplers = lax.all_gather(coupler_part, "head", axis=1, tiled=True)
    token_count = inputs.shape[0]
    state_heads = inputs.shape[1] // HDIM
    inputs_wide = inputs.astype(jnp.float32).reshape(token_count, state_heads, HDIM)
    c_rows = couplers[:, NSTATE:]
    within, growth, total_decay, end_state = block_terms(
        inputs_wide, couplers[:, :NSTATE], c_rows, decay
    )
    identity = (jnp.ones_like(total_decay), jnp.zeros_like(end_state))
    incoming = prefix((total_decay, end_state), "tm", combine_states, identity)
    from_state = jnp.einsum(
        "tn,hpn->thp", c_rows.astype(jnp.float32), incoming[1], precision=HIGHEST
    )
    result_rows = within + growth[:, :, None] * from_state + skip_gain[None, :, None] * inputs_wide
    mixed = result_rows.astype(jnp.bfloat16).reshape(token_count, state_heads * HDIM)
    return (encoded, mixed)


def solution(mesh):
    placed = (
        P("tm", "head"),
        P(),
        P(),
        P(),
        P(None, None, "head"),
        P(None, "head"),
        P("head"),
        P("head", None),
        P(),
        P(None, "head"),
        P(None, "head"),
        P("tm", "head"),
        P("head"),
    )
    return jax.shard_map(
        per_device,
        mesh=mesh,
        in_specs=placed,
        out_specs=(P("tm", "head"), P("tm", "head")),
        check_vma=False,
    )
```

profile of v0, /device:TPU:27, one launch (start us, length us, event | category | flops | bytes accessed | tf_op | source)
XLA Modules:
  0.0 243.5 jit_solution(4157910244841863464)
XLA Ops:
  7.2 9.6 %all_gather.25 = bf16[256,1280]{1,0:T(8,128)(2,1)S(1)} all-gather(bf16[256,640]{1,0:T(8,128)(2,1)} %param.15), channel_id=1, replica_groups=mesh['tm'=16,'head'=2] {'head'}, dimensions={1}, use_global_device_ids=true | all-gather | bytes 983040 | tf_op jit(solution)/shard_map/all_gather | solution.py:91
  17.3 1.9 fusion.29
  19.3 1.9 fusion.26
  21.2 3.5 %collective-permute-start.1 = (bf16[256,1024]{1,0:T(8,128)(2,1)S(1)}, bf16[256,1024]{1,0:T(8,128)(2,1)S(1)}, u32[]{:S(2)}, u32[]{:S(2)}) collective-permute-start(bf16[256,1024]{1,0:T(8,128)(2,1)S(1)} %pad_maximum_fusion.1), channel_id=1, source_target_pairs={{2,0},{4,2},{6,4},{8,6},{10,8},{12,10},{14,12},{16,14},{18,16},{20... | collective-permute-start | bytes 1572872 | tf_op jit(solution)/shard_map/ppermute | solution.py:26
  24.7 1.3 collective-permute-start
  26.0 5.7 %copy.58 = bf16[640,2560]{0,1:T(8,128)(2,1)} copy(bf16[640,2560]{1,0:T(8,128)(2,1)} %param.22) | data formatting | bytes 6553600 | tf_op args[7]
  31.7 5.2 %all-to-all-start = ((bf16[640,2,1280]{0,2,1:T(8,128)(2,1)}), bf16[640,2,1280]{0,2,1:T(8,128)(2,1)}, u32[]{:S(2)}, u32[]{:S(2)}) async-start(bf16[640,2,1280]{0,2,1:T(8,128)(2,1)} %bitcast.67), calls=%async_computation | async-start | bytes 6553600 | tf_op jit(solution)/shard_map/all_to_all | solution.py:90
  37.0 2.6 %fusion.32 = bf16[256,512]{1,0:T(8,128)(2,1)} fusion(bf16[3,1280,512]{2,1,0:T(8,128)(2,1)} %param.19, bf16[256,1280]{1,0:T(8,128)(2,1)S(1)} %all_gather.25, f32[1280]{0:T(1024)} %param.18, f32[1280]{0:T(1024)} %param.17, f32[256]{0:T(256)} %copy-done.18, f32[256]{0:T(256)} %copy-done.17), kind=kOutput, calls=%fused_computation.39 | convolution fusion | flops 337641472 | bytes 2246656 | tf_op jit(solution)/shard_map/dot_general | solution.py:93
  39.7 0.7 broadcast_subtract_fusion
  40.4 0.7 copy.60
  41.9 1.8 copy.56
  43.7 1.4 dynamic_slice.28
  45.8 0.9 broadcast_compare_fusion
  46.6 1.2 pad_maximum_fusion
  48.0 1.2 copy.57
  49.2 6.1 %fusion.66 = (f32[8,256]{1,0:T(8,128)S(1)}, f32[8,256,768]{2,1,0:T(8,128)}) fusion(pred[256,768]{1,0:T(8,128)(4,1)S(1)} %copy-done.9, bf16[256,8,64]{0,2,1:T(8,128)(2,1)S(1)} %bitcast.74, bf16[768,8,64]{0,2,1:T(8,128)(2,1)} %bitcast.71), kind=kOutput, calls=%fused_computation.86 | convolution fusion | flops 207618816 | bytes 7544832 | tf_op jit(solution)/shard_map/while/body/eval_jaxpr/sub | solution.py:127
  55.6 4.0 %fusion.35 = bf16[8,64,256]{2,1,0:T(8,128)(2,1)S(1)} fusion(bf16[768,8,64]{0,2,1:T(8,128)(2,1)S(1)} %bitcast.72, f32[8,256,768]{2,1,0:T(8,128)} %get-tuple-element.94, f32[8,256]{1,0:T(8,128)S(1)} %get-tuple-element.93), kind=kOutput, calls=%fused_computation.40 | convolution fusion | flops 204603392 | bytes 7348224 | tf_op jit(solution)/shard_map/while/body/eval_jaxpr/hqk,khe->qhe/dot_general | solution.py:129
  59.6 19.3 %all_gather.26 = bf16[256,1024]{0,1:T(8,128)(2,1)S(1)} all-gather(bf16[256,512]{0,1:T(8,128)(2,1)S(1)} %bitcast.73), channel_id=1, replica_groups=mesh['tm'=16,'head'=2] {'head'}, dimensions={1}, use_global_device_ids=true | all-gather | bytes 786432 | tf_op jit(solution)/shard_map/all_gather | solution.py:136
  79.5 0.7 copy-done.3
  80.8 4.0 %all_gather.27 = bf16[64,1280]{1,0:T(8,128)(2,1)S(1)} all-gather(bf16[64,640]{1,0:T(8,128)(2,1)S(1)} %multiply_convert_fusion.2), channel_id=1, replica_groups=mesh['tm'=16,'head'=2] {'head'}, dimensions={1}, use_global_device_ids=true | all-gather | bytes 245760 | tf_op jit(solution)/shard_map/all_gather | solution.py:144
  84.8 5.6 %copy.59 = bf16[2,640,1280]{2,1,0:T(8,128)(2,1)} copy(bf16[2,640,1280]{1,2,0:T(8,128)(2,1)} %bitcast.11) | data formatting | bytes 6553600 | tf_op jit(solution)/shard_map/all_to_all | solution.py:90
  90.4 2.8 %multiply_reduce_fusion = (f32[64]{0:T(128)S(1)}, f32[64,1280]{1,0:T(8,128)S(1)}) fusion(bf16[64,1280]{1,0:T(8,128)(2,1)S(1)} %all_gather.27, bf16[1280,1280]{1,0:T(8,128)(2,1)} %bitcast.68), kind=kOutput, calls=%fused_computation.59 | convolution fusion | flops 209878976 | bytes 3768576 | tf_op jit(solution)/shard_map/dot_general | solution.py:145
  93.2 3.8 %psum.7 = f32[64]{0:T(128)S(1)} all-reduce(f32[64]{0:T(128)S(1)} %get-tuple-element.95), channel_id=1, replica_groups=mesh['tm'=16,'head'=2] {'head'}, use_global_device_ids=true, to_apply=%region_6.7 | all-reduce | flops 64 | bytes 512 | tf_op jit(solution)/shard_map/psum | solution.py:147
  97.1 4.9 %all_gather.28 = bf16[64,2560]{1,0:T(8,128)(2,1)S(1)} all-gather(bf16[64,1280]{1,0:T(8,128)(2,1)S(1)} %multiply_convert_fusion.1), channel_id=1, replica_groups=mesh['tm'=16,'head'=2] {'head'}, dimensions={1}, use_global_device_ids=true | all-gather | bytes 491520 | tf_op jit(solution)/shard_map/all_gather | solution.py:154
  102.3 4.2 %fusion.50 = f32[64,1280]{1,0:T(8,128)S(1)} fusion(bf16[64,2560]{1,0:T(8,128)(2,1)S(1)} %all_gather.28, bf16[2560,1280]{1,0:T(8,128)(2,1)} %param.24), kind=kOutput, calls=%fused_computation.61 | convolution fusion | flops 419921920 | bytes 7208960 | tf_op jit(solution)/shard_map/dot_general | solution.py:155
  106.5 3.5 %all_gather.29 = bf16[64,256]{1,0:T(8,128)(2,1)S(1)} all-gather(bf16[64,128]{1,0:T(8,128)(2,1)S(1)} %multiply_convert_fusion.3), channel_id=1, replica_groups=mesh['tm'=16,'head'=2] {'head'}, dimensions={1}, use_global_device_ids=true | all-gather | bytes 49152 | tf_op jit(solution)/shard_map/all_gather | solution.py:161
  110.7 1.5 fusion.36
  113.1 24.0 %all-gather.1 = f32[16,1,20]{2,1,0:T(1,128)} all-gather(f32[1,1,20]{2,1,0:T(1,128)S(1)} %copy-done.20), channel_id=1, replica_groups=mesh['tm'=16,'head'=2] {'tm'}, dimensions={0}, use_global_device_ids=true | all-gather | bytes 1360 | tf_op jit(solution)/shard_map/all_gather | solution.py:33
  137.9 0.9 fusion.54
  138.8 65.7 %all-gather.4.cloned.1.call-done = f32[320,64,128]{2,1,0:T(8,128)} async-done(((f32[20,64,128]{2,1,0:T(8,128)}), f32[320,64,128]{2,1,0:T(8,128)}) %all-gather.4.cloned.1.call-update) | async-done | bytes 10485776 | tf_op jit(solution)/shard_map/all_gather | solution.py:33
  204.6 29.3 %while.3 = (s32[]{:T(128)}, f32[20,64,128]{2,1,0:T(8,128)S(1)}, s32[]{:T(128)}, f32[16,20]{1,0:T(8,128)}, f32[16,20,64,128]{3,2,1,0:T(8,128)}, /*index=5*/s32[]{:T(128)}, s32[]{:T(128)}, s32[]{:T(128)}) while((s32[]{:T(128)}, f32[20,64,128]{2,1,0:T(8,128)S(1)}, s32[]{:T(128)}, f32[16,20]{1,0:T(8,128)}, f32[16,20,64,128]{3,2,1,0:T(8,128)}, ...), condition=%wide.region_9.10_spmd, body=%wide.region_8.9_spmd.sunk | while | flops 327685 | bytes 1966455 | solution.py:41
  205.3 1.2 bitcast_add_fusion.2
  207.3 1.2 bitcast_add_fusion.2
  209.2 1.2 bitcast_add_fusion.2
  211.2 1.2 bitcast_add_fusion.2
  213.1 1.2 bitcast_add_fusion.2
  215.1 1.2 bitcast_add_fusion.2
  217.0 1.2 bitcast_add_fusion.2
  219.0 1.2 bitcast_add_fusion.2
  220.9 1.2 bitcast_add_fusion.2
  222.9 1.2 bitcast_add_fusion.2
  224.9 1.2 bitcast_add_fusion.2
  226.8 1.2 bitcast_add_fusion.2
  228.8 1.2 bitcast_add_fusion.2
  230.7 1.2 bitcast_add_fusion.2
  232.7 1.2 bitcast_add_fusion.2
  234.4 1.4 fusion.24
  235.9 0.8 copy.69
  (95 shorter events, 17.2 us)
Async XLA Ops:
  7.2 71.7 %copy-start = (bf16[1024,640]{1,0:T(8,128)(2,1)S(1)}, bf16[1024,640]{1,0:T(8,128)(2,1)}, u32[]{:S(2)}) copy-start(bf16[1024,640]{1,0:T(8,128)(2,1)} %param.20) | copy-start | bytes 3932164
  7.2 10.1 %copy-start.21 = (f32[1280]{0:T(1024)S(1)}, f32[1280]{0:T(1024)}, u32[]{:S(2)}) copy-start(f32[1280]{0:T(1024)} %param.18) | copy-start | bytes 15364
  7.2 10.1 %copy-start.22 = (f32[1280]{0:T(1024)S(1)}, f32[1280]{0:T(1024)}, u32[]{:S(2)}) copy-start(f32[1280]{0:T(1024)} %param.17) | copy-start | bytes 15364
  17.0 2.3 copy-start.17
  17.3 1.9 copy-start.18
  21.2 25.4 %collective-permute-start.1 = (bf16[256,1024]{1,0:T(8,128)(2,1)S(1)}, bf16[256,1024]{1,0:T(8,128)(2,1)S(1)}, u32[]{:S(2)}, u32[]{:S(2)}) collective-permute-start(bf16[256,1024]{1,0:T(8,128)(2,1)S(1)} %pad_maximum_fusion.1), channel_id=1, source_target_pairs={{2,0},{4,2},{6,4},{8,6},{10,8},{12,10},{14,12},{16,14},{18,16},{20... | collective-permute-start | bytes 1572872 | tf_op jit(solution)/shard_map/ppermute | solution.py:26
  24.7 21.9 %collective-permute-start = (bf16[256,1024]{1,0:T(8,128)(2,1)S(1)}, bf16[256,1024]{1,0:T(8,128)(2,1)}, u32[]{:S(2)}, u32[]{:S(2)}) collective-permute-start(bf16[256,1024]{1,0:T(8,128)(2,1)S(1)} %pad_maximum_fusion.1), channel_id=1, source_target_pairs={{0,2},{2,4},{4,6},{6,8},{8,10},{10,12},{12,14},{14,16},{16,18},{18... | collective-permute-start | bytes 1572872 | tf_op jit(solution)/shard_map/ppermute | solution.py:23
  31.7 53.1 %all-to-all-start = ((bf16[640,2,1280]{0,2,1:T(8,128)(2,1)}), bf16[640,2,1280]{0,2,1:T(8,128)(2,1)}, u32[]{:S(2)}, u32[]{:S(2)}) async-start(bf16[640,2,1280]{0,2,1:T(8,128)(2,1)} %bitcast.67), calls=%async_computation | async-start | bytes 6553600 | tf_op jit(solution)/shard_map/all_to_all | solution.py:90
  36.9 167.6 %all-gather.4.cloned.1.call-start = ((), (), s32[]{:S(2)}) async-start(), calls=%async_computation.1 | async-start | bytes 11141120 | tf_op jit(solution)/shard_map/all_gather | solution.py:33
  37.0 2.6 %copy-start.13 = (s32[4096]{0:T(1024)S(1)}, s32[4096]{0:T(1024)}, u32[]{:S(2)}) copy-start(s32[4096]{0:T(1024)} %param.16) | copy-start | bytes 49156
  41.3 5.4 %copy-start.4 = (f32[64,20]{1,0:T(8,128)}, f32[64,20]{1,0:T(8,128)S(1)}, u32[]{:S(2)}) copy-start(f32[64,20]{1,0:T(8,128)S(1)} %reduce_window_sum.11) | copy-start | bytes 15364
  47.9 1.2 copy-start.8
  48.0 1.2 copy-start.9
  55.6 23.3 %copy-start.2 = (bf16[256,640]{1,0:T(8,128)(2,1)S(1)}, bf16[256,640]{1,0:T(8,128)(2,1)}, u32[]{:S(2)}) copy-start(bf16[256,640]{1,0:T(8,128)(2,1)} %param.15) | copy-start | bytes 983044
  55.6 23.3 %copy-start.23 = (f32[640]{0:T(1024)S(1)}, f32[640]{0:T(1024)}, u32[]{:S(2)}) copy-start(f32[640]{0:T(1024)} %param.21) | copy-start | bytes 7684
  79.5 0.7 copy-start.3
  90.4 6.6 %copy-start.15 = (f32[1280]{0:T(1024)S(1)}, f32[1280]{0:T(1024)}, u32[]{:S(2)}) copy-start(f32[1280]{0:T(1024)} %dynamic_slice.28) | copy-start | bytes 15364
  90.4 11.6 %copy-start.1 = (bf16[2560,128]{1,0:T(8,128)(2,1)S(1)}, bf16[2560,128]{1,0:T(8,128)(2,1)}, u32[]{:S(2)}) copy-start(bf16[2560,128]{1,0:T(8,128)(2,1)} %param.25) | copy-start | bytes 1966084
  102.3 7.9 %copy-start.10 = (f32[64,20]{1,0:T(8,128)S(1)}, f32[64,20]{1,0:T(8,128)}, u32[]{:S(2)}) copy-start(f32[64,20]{1,0:T(8,128)} %get-tuple-element.88) | copy-start | bytes 15364
  102.3 7.9 %copy-start.11 = (f32[64,20]{1,0:T(8,128)S(1)}, f32[64,20]{1,0:T(8,128)}, u32[]{:S(2)}) copy-start(f32[64,20]{1,0:T(8,128)} %copy.60) | copy-start | bytes 15364
  110.0 0.7 copy-start.6
  110.7 1.6 copy-start.5
  110.7 1.7 copy-start.12
  110.7 2.4 copy-start.20
  204.5 29.4 %copy-start.7 = (bf16[64,256]{1,0:T(8,128)(2,1)S(1)}, bf16[64,256]{1,0:T(8,128)(2,1)}, u32[]{:S(2)}) copy-start(bf16[64,256]{1,0:T(8,128)(2,1)} %copy-done.6) | copy-start | bytes 98308
  204.6 29.4 %copy-start.14 = (f32[64,20]{0,1:T(8,128)S(1)}, f32[64,20]{0,1:T(8,128)}, u32[]{:S(2)}) copy-start(f32[64,20]{0,1:T(8,128)} %copy.65) | copy-start | bytes 15364
  204.6 29.8 %copy-start.16 = (pred[64,64]{1,0:T(8,128)(4,1)S(1)}, pred[64,64]{1,0:T(8,128)(4,1)}, u32[]{:S(2)}) copy-start(pred[64,64]{1,0:T(8,128)(4,1)} %iota_compare_fusion) | copy-start | bytes 12292
  204.6 29.8 %copy-start.19 = (f32[20]{0:T(128)S(1)}, f32[20]{0:T(128)}, u32[]{:S(2)}) copy-start(f32[20]{0:T(128)} %param.27) | copy-start | bytes 244
Sparse Core Ops, SparseCore 0:
  112.4 92.0 all-gather.3
where the time goes:
time: 246 us; the launch traced here: 244 us
  blocking collectives  69 us (28%)
  waiting for transfers between devices  65.7 us (27%)
  local copies, waits for them, and re-layouts  31 us (13%)
  matrix products  28.6 us (12%)
  other arithmetic  24.3 us (10%)
  between operations  14.5 us (6%)
  starting transfers between devices  10.1 us (4%)
    all_gather x1, waiting for transfers between devices, prefix(): gathered = jax.tree.map(lambda a: lax.all_gather(a, axis), part)  65.7 us
    all_gather x1, blocking collectives, prefix(): gathered = jax.tree.map(lambda a: lax.all_gather(a, axis), part)  24 us
    all_gather x1, blocking collectives, per_device(): lax.all_gather(attended, 'head', axis=1, tiled=True)  19.3 us
    add x15, other arithmetic, combine_states(): later[0][:, None, None] * earlier[1] + later[1]  18.7 us
    mul x15, local copies, waits for them, and re-layouts, combine_states(): later[0][:, None, None] * earlier[1] + later[1]  10.3 us
    all_gather x1, blocking collectives, per_device(): gathered = lax.all_gather(frames, 'head', axis=1, tiled=True)  9.6 us
    unnamed x50, local copies, waits for them, and re-layouts  7.33 us
    sub x1, matrix products, attend(): raised = jnp.exp(scores - peak)  6.11 us
  transfers between devices with their start and end apart: 4, of which 1 were waited for; matrix products, arithmetic and copies ran while one was open for 13% of the time, Pallas kernels for 0%

commit v1 on v0

--- a/solution.py
+++ b/solution.py
@@ -1,8 +1,11 @@
+import functools
 import math
 
 import jax
 import jax.numpy as jnp
 from jax import lax
+from jax.experimental import pallas as pl
+from jax.experimental.pallas import tpu as pltpu
 from jax.sharding import PartitionSpec as P
 
 EHEAD_DIM = 64
@@ -176,6 +179,432 @@
     return (encoded, mixed)
 
 
+PLANE = 4
+MESH = pl.DeviceIdType.MESH
+VM = pl.BlockSpec(memory_space=pltpu.VMEM)
+HB = pl.BlockSpec(memory_space=pl.ANY)
+F32 = jnp.float32
+BF16 = jnp.bfloat16
+NT = (((1,), (1,)), ((), ()))
+TN = (((0,), (0,)), ((), ()))
+
+
+def dot(a, b, dims=(((1,), (0,)), ((), ())), precision=None):
+    return lax.dot_general(a, b, dims, precision=precision, preferred_element_type=F32)
+
+
+def iota(shape, dim):
+    return lax.broadcasted_iota(jnp.int32, shape, dim)
+
+
+def fused_kernel(
+    nt,
+    frames, ids, ln_gain, ln_bias, qkv_hbm, out_hbm, out_bias, ad_hbm, rms_gain, x_hbm, bc_hbm, decay, skip,
+    enc_o, mix_o,
+    wqkv, wout, wad, wx, wbc, wsem,
+    fb, nb, qb, kb, vb, mk, acc, mb, lb, att, pf, ps, pr, sc, cp, xin, xq, xb, bcb, db,
+    sm, sb, inc, yacc, yb, yr, send, recv,
+):
+    tm = lax.axis_index("tm")
+    hy = lax.axis_index("head")
+    z = tm // PLANE
+    q = tm % PLANE
+    planes = nt // PLANE
+    rows = frames.shape[0]
+    half = frames.shape[1]
+    toks = decay.shape[0]
+    span = PLANE * toks
+    width = qb.shape[1]
+    pairs = width // 128
+    qw = xb.shape[2]
+    qheads = qw // HDIM
+    heads = decay.shape[1]
+
+    loads = [
+        pltpu.make_async_copy(src, dst, wsem.at[i])
+        for i, (src, dst) in enumerate(
+            [
+                (qkv_hbm.at[1], wqkv.at[1]),
+                (qkv_hbm.at[2], wqkv.at[2]),
+                (qkv_hbm.at[0], wqkv.at[0]),
+                (out_hbm, wout),
+                (ad_hbm, wad),
+                (bc_hbm, wbc),
+                (x_hbm, wx),
+            ]
+        )
+    ]
+
+    def remote(src, dst, sem, device):
+        return pltpu.make_async_remote_copy(
+            src_ref=src, dst_ref=dst, send_sem=send.at[sem], recv_sem=recv.at[sem],
+            device_id=device, device_id_type=MESH,
+        )
+
+    partner = {"head": 1 - hy}
+    peers = [{"tm": z * PLANE + (q + k) % PLANE} for k in range(1, PLANE)]
+    prev = {"tm": (tm + nt - 1) % nt}
+    after = {"tm": (tm + 1) % nt}
+    bar = pltpu.get_barrier_semaphore()
+
+    def greet(device):
+        pl.semaphore_signal(bar, inc=1, device_id=device, device_id_type=MESH)
+
+    greet(partner)
+    for peer in peers:
+        greet(peer)
+    for dz in range(1, planes):
+        greet({"tm": (tm + dz * PLANE) % nt})
+    cross_prev = jnp.logical_and(q == 0, tm > 0)
+    cross_next = jnp.logical_and(q == PLANE - 1, tm < nt - 1)
+
+    @pl.when(cross_prev)
+    def _():
+        greet(prev)
+
+    @pl.when(cross_next)
+    def _():
+        greet(after)
+
+    for load in loads:
+        load.start()
+    fb[hy] = frames[...]
+    db[q] = decay[...]
+    pl.semaphore_wait(bar, PLANE + planes - 1 + cross_prev.astype(jnp.int32) + cross_next.astype(jnp.int32))
+
+    c_frames = remote(frames, fb.at[hy], 0, partner)
+    c_frames.start()
+    c_decay = [remote(decay, db.at[q], k + 1, peer) for k, peer in enumerate(peers)]
+    for c in c_decay:
+        c.start()
+
+    own = ids[pl.ds(tm, 1), :].astype(F32)
+    low = jnp.where(tm > 0, ids[pl.ds((tm + nt - 1) % nt, 1), :].astype(F32), -1.0)
+    high = jnp.where(tm < nt - 1, ids[pl.ds((tm + 1) % nt, 1), :].astype(F32), -1.0)
+    own_col = jnp.transpose(jnp.broadcast_to(own, (128, rows)))[:, :1]
+    for i, row in enumerate((own, low, high)):
+        mk[:, i * rows : (i + 1) * rows] = jnp.where(own_col == row, 0.0, -1e30)
+
+    @pl.when(tm == 0)
+    def _():
+        kb[1] = jnp.zeros((rows, width), BF16)
+        vb[1] = jnp.zeros((rows, width), BF16)
+
+    @pl.when(tm == nt - 1)
+    def _():
+        kb[2] = jnp.zeros((rows, width), BF16)
+        vb[2] = jnp.zeros((rows, width), BF16)
+
+    c_frames.wait()
+    both = jnp.concatenate([fb[0], fb[1]], axis=1).astype(F32)
+    center = jnp.mean(both, axis=-1, keepdims=True)
+    moved = both - center
+    spread = jnp.mean(jnp.square(moved), axis=-1, keepdims=True)
+    nb[...] = (moved * lax.rsqrt(spread + EPSILON) * ln_gain[...] + ln_bias[...]).astype(BF16)
+
+    def project(which, dst, scale):
+        def tile(j, carry):
+            cols = pl.ds(pl.multiple_of(j * 256, 256), 256)
+            part = dot(nb[...], wqkv[which, :, cols]).astype(BF16)
+            dst[:, cols] = part * scale if scale is not None else part
+            return carry
+
+        lax.fori_loop(0, width // 256, tile, 0)
+
+    def halo(buf, sem):
+        return (remote(buf.at[0], buf.at[1], sem, after), remote(buf.at[0], buf.at[2], sem + 1, prev))
+
+    def halo_start(pair):
+        @pl.when(tm < nt - 1)
+        def _():
+            pair[0].start()
+
+        @pl.when(tm > 0)
+        def _():
+            pair[1].start()
+
+    def halo_wait(pair):
+        @pl.when(tm > 0)
+        def _():
+            pair[0].wait_recv()
+            pair[1].wait_send()
+
+        @pl.when(tm < nt - 1)
+        def _():
+            pair[0].wait_send()
+            pair[1].wait_recv()
+
+    loads[0].wait()
+    project(1, kb.at[0], None)
+    c_k = halo(kb, 4)
+    halo_start(c_k)
+    loads[1].wait()
+    project(2, vb.at[0], None)
+    c_v = halo(vb, 6)
+    halo_start(c_v)
+    loads[2].wait()
+    project(0, qb, jnp.asarray(EHEAD_DIM ** (-0.5), BF16))
+
+    lane = iota((1, 128), 1)
+    is_low = lane < EHEAD_DIM
+    sides = (jnp.where(is_low, 1.0, 0.0).astype(BF16), jnp.where(is_low, 0.0, 1.0).astype(BF16))
+
+    def within_own(p, carry):
+        cols = pl.ds(pl.multiple_of(p * 128, 128), 128)
+        qp, kp, vp = qb[:, cols], kb[0, :, cols], vb[0, :, cols]
+        got = []
+        for side in sides:
+            s = dot(qp * side, kp, NT) + mk[:, :rows]
+            m = jnp.max(s, axis=-1, keepdims=True)
+            e = jnp.exp(s - m)
+            got.append((dot(e.astype(BF16), vp), m, jnp.sum(e, axis=-1, keepdims=True)))
+        acc[p] = jnp.where(is_low, got[0][0], got[1][0])
+        mb[p] = jnp.where(is_low, got[0][1], got[1][1])
+        lb[p] = jnp.where(is_low, got[0][2], got[1][2])
+        return carry
+
+    lax.fori_loop(0, pairs, within_own, 0)
+    halo_wait(c_k)
+    halo_wait(c_v)
+
+    def att_copy(p):
+        cols = pl.ds(pl.multiple_of(hy * width + p * 128, 128), 128)
+        return remote(att.at[:, cols], att.at[:, cols], 8 + p, partner)
+
+    def with_halos(p, carry):
+        cols = pl.ds(pl.multiple_of(p * 128, 128), 128)
+        qp = qb[:, cols]
+        kp = kb[1:3, :, cols].reshape(2 * rows, 128)
+        vp = vb[1:3, :, cols].reshape(2 * rows, 128)
+        old_m, old_l = mb[p], lb[p]
+        got = []
+        for i, side in enumerate(sides):
+            s = dot(qp * side, kp, NT) + mk[:, rows:]
+            m1 = old_m[:, i * EHEAD_DIM : i * EHEAD_DIM + 1]
+            m = jnp.maximum(jnp.max(s, axis=-1, keepdims=True), m1)
+            e = jnp.exp(s - m)
+            got.append((dot(e.astype(BF16), vp), m, jnp.sum(e, axis=-1, keepdims=True)))
+        fade = jnp.exp(old_m - jnp.where(is_low, got[0][1], got[1][1]))
+        total = old_l * fade + jnp.where(is_low, got[0][2], got[1][2])
+        blended = acc[p] * fade + jnp.where(is_low, got[0][0], got[1][0])
+        att[:, pl.ds(pl.multiple_of(hy * width + p * 128, 128), 128)] = (blended / total).astype(BF16)
+        att_copy(p).start()
+        return carry
+
+    lax.fori_loop(0, pairs, with_halos, 0)
+    for p in range(pairs):
+        att_copy(p).wait()
+
+    loads[3].wait()
+    encoded = (frames[...].astype(F32) + dot(att[...], wout[...]) + out_bias[...]).astype(BF16)
+    enc_o[...] = encoded
+    rr, cc = iota((toks, rows), 0) * 4, iota((toks, rows), 1)
+    pool = jnp.where(jnp.logical_and(cc >= rr, cc < rr + 4), 0.25, 0.0).astype(BF16)
+    pooled = dot(pool, encoded).astype(BF16)
+
+    loads[4].wait()
+
+    def adapt(j, carry):
+        cols = pl.ds(pl.multiple_of(j * 256, 256), 256)
+        part = dot(pooled, wad[:, cols])
+        pf[:, cols] = part
+        ps[:, cols] = part.astype(BF16)
+        return carry
+
+    lax.fori_loop(0, wad.shape[1] // 256, adapt, 0)
+    c_part = remote(ps, pr, 12, partner)
+    c_part.start()
+
+    for c in c_decay:
+        c.wait()
+    dec = db[...].reshape(span, heads)
+    picked_row = q * qheads
+    sel = jnp.where(iota((heads, 128), 0) == picked_row + iota((heads, 128), 1), 1.0, 0.0)
+    sel = jnp.where(iota((heads, 128), 1) < qheads, sel, 0.0)
+    first = (iota((heads, qw), 0) - picked_row) * HDIM
+    wide = iota((heads, qw), 1)
+    expand = jnp.where(jnp.logical_and(wide >= first, wide < first + HDIM), 1.0, 0.0)
+    tri = jnp.where(iota((span, span), 0) >= iota((span, span), 1), 1.0, 0.0)
+    cum = dot(tri, jnp.log(jnp.maximum(dec, 1e-37)), precision=HIGHEST)
+    cum_col = dot(cum, sel, precision=HIGHEST)
+    cum_row = jnp.transpose(cum_col)
+    growth = dot(jnp.exp(cum), expand, precision=HIGHEST)
+    tail = dot(jnp.exp(cum[span - 1 :, :] - cum), expand, precision=HIGHEST)
+    drive = dot(1.0 - dec, expand, precision=HIGHEST)
+    skip_wide = dot(jnp.broadcast_to(skip[...], (8, heads)), expand, precision=HIGHEST)[:1, :]
+    total = growth[span - 1 :, :]
+    t0 = total.astype(BF16).astype(F32)
+    t1 = (total - t0).astype(BF16).astype(F32)
+    t2 = total - t0 - t1
+    r16 = iota((16, qw), 0)
+    sm[NSTATE:, :] = jnp.where(r16 == 0, t0, jnp.where(r16 == 1, t1, jnp.where(r16 == 2, t2, 0.0))).astype(BF16)
+
+    c_part.wait()
+    proj = pf[...] + pr[...].astype(F32)
+    square = jnp.mean(jnp.square(proj), axis=-1, keepdims=True)
+    sc[...] = (proj * lax.rsqrt(square + EPSILON) * rms_gain[...]).astype(BF16)
+
+    def silu(v):
+        return v / (1.0 + jnp.exp(-v))
+
+    loads[5].wait()
+    cp[hy] = silu(dot(sc[...], wbc[...])).astype(BF16)
+    c_cp = remote(cp.at[hy], cp.at[hy], 13, partner)
+    c_cp.start()
+    loads[6].wait()
+
+    def drive_in(j, carry):
+        cols = pl.ds(pl.multiple_of(j * 256, 256), 256)
+        xin[:, cols] = silu(dot(sc[...], wx[:, cols]))
+        return carry
+
+    lax.fori_loop(0, wx.shape[1] // 256, drive_in, 0)
+    for j in range(PLANE):
+        xq[j] = xin[:, j * qw : (j + 1) * qw].astype(BF16)
+    c_x = [remote(xq.at[(q + k) % PLANE], xb.at[q], 13 + k, peers[k - 1]) for k in range(1, PLANE)]
+    for c in c_x:
+        c.start()
+    xb[q] = xq[q]
+    c_cp.wait()
+    c_bc = [remote(cp, bcb.at[:, q], 16 + k, peers[k - 1]) for k in range(1, PLANE)]
+    for c in c_bc:
+        c.start()
+    bcb[:, q] = cp[...]
+    for c in c_x:
+        c.wait()
+    for c in c_bc:
+        c.wait()
+
+    x_all = xb[...].reshape(span, qw).astype(F32)
+    b_all = bcb[0].reshape(span, NSTATE)
+    c_all = bcb[1].reshape(span, NSTATE)
+    driven = x_all * drive
+    sm[:NSTATE, :] = dot(b_all, (driven * tail).astype(BF16), TN).astype(BF16)
+
+    def state_copy(dz):
+        return remote(sm, sb.at[z], 19 + dz, {"tm": (tm + dz * PLANE) % nt})
+
+    for dz in range(1, planes):
+        @pl.when(z + dz < planes)
+        def _():
+            state_copy(dz).start()
+
+    affinity = dot(c_all, b_all, NT)
+    causal = iota((span, span), 0) >= iota((span, span), 1)
+    driven = driven.astype(BF16)
+
+    def head_out(h, cols):
+        gap = cum_col[:, h : h + 1] - cum_row[h : h + 1, :]
+        mixing = affinity * jnp.exp(jnp.where(causal, gap, -1e30))
+        return dot(mixing.astype(BF16), cols)
+
+    for h in range(0, qheads, 2):
+        if h + 1 < qheads:
+            cols = driven[:, h * HDIM : (h + 2) * HDIM]
+            yacc[:, h * HDIM : (h + 2) * HDIM] = jnp.where(is_low, head_out(h, cols), head_out(h + 1, cols))
+        else:
+            yacc[:, h * HDIM : (h + 1) * HDIM] = head_out(h, driven[:, h * HDIM : (h + 1) * HDIM])
+    yacc[...] = yacc[...] + skip_wide * x_all
+
+    inc[...] = jnp.zeros(inc.shape, F32)
+    for zp in range(planes - 1):
+        @pl.when(zp < z)
+        def _():
+            pltpu.make_async_remote_copy(
+                src_ref=sm, dst_ref=sb.at[zp], send_sem=send.at[19 + z - zp], recv_sem=recv.at[19 + z - zp],
+                device_id=partner, device_id_type=MESH,
+            ).wait_recv()
+            got = sb[zp].astype(F32)
+            fade = got[NSTATE : NSTATE + 1] + got[NSTATE + 1 : NSTATE + 2] + got[NSTATE + 2 : NSTATE + 3]
+            inc[...] = inc[...] * fade + got[:NSTATE]
+
+    y = yacc[...] + growth * dot(c_all, inc[...].astype(BF16))
+    yb[...] = y.astype(BF16).reshape(PLANE, toks, qw)
+    base = 19 + planes
+    c_y = [remote(yb.at[(q + k) % PLANE], yr.at[q], base + k - 1, peers[k - 1]) for k in range(1, PLANE)]
+    for c in c_y:
+        c.start()
+    yr[q] = yb[q]
+    for dz in range(1, planes):
+        @pl.when(z + dz < planes)
+        def _():
+            state_copy(dz).wait_send()
+    for c in c_y:
+        c.wait()
+    mix_o[...] = yr[...]
+
+
+def fused(nt):
+    def per_device(frames, segment_ids, ln_gain, ln_bias, qkv_weight, out_weight, out_bias, adapter, rms_gain,
+                   x_weight, bc_weight, decay, skip_gain):
+        rows, half = frames.shape
+        width = qkv_weight.shape[2]
+        toks, heads = decay.shape
+        dm = adapter.shape[1]
+        xw = x_weight.shape[1]
+        qw = xw // PLANE
+        planes = nt // PLANE
+        span = PLANE * toks
+        pairs = width // 128
+        sems = 19 + planes + PLANE - 1
+        v = pltpu.VMEM
+        encoded, mixed = pl.pallas_call(
+            functools.partial(fused_kernel, nt),
+            out_shape=(
+                jax.ShapeDtypeStruct((rows, half), BF16),
+                jax.ShapeDtypeStruct((PLANE, toks, qw), BF16),
+            ),
+            in_specs=[VM, VM, VM, VM, HB, HB, VM, HB, VM, HB, HB, VM, VM],
+            out_specs=(VM, VM),
+            scratch_shapes=[
+                v(qkv_weight.shape, BF16),
+                v(out_weight.shape, BF16),
+                v(adapter.shape, BF16),
+                v(x_weight.shape, BF16),
+                v(bc_weight.shape, BF16),
+                pltpu.SemaphoreType.DMA((7,)),
+                v((2, rows, half), BF16),
+                v((rows, 2 * half), BF16),
+                v((rows, width), BF16),
+                v((3, rows, width), BF16),
+                v((3, rows, width), BF16),
+                v((rows, 3 * rows), F32),
+                v((pairs, rows, 128), F32),
+                v((pairs, rows, 128), F32),
+                v((pairs, rows, 128), F32),
+                v((rows, 2 * width), BF16),
+                v((toks, dm), F32),
+                v((toks, dm), BF16),
+                v((toks, dm), BF16),
+                v((toks, dm), BF16),
+                v((2, toks, NSTATE), BF16),
+                v((toks, xw), F32),
+                v((PLANE, toks, qw), BF16),
+                v((PLANE, toks, qw), BF16),
+                v((2, PLANE, toks, NSTATE), BF16),
+                v((PLANE, toks, heads), F32),
+                v((NSTATE + 16, qw), BF16),
+                v((planes, NSTATE + 16, qw), BF16),
+                v((NSTATE, qw), F32),
+                v((span, qw), F32),
+                v((PLANE, toks, qw), BF16),
+                v((PLANE, toks, qw), BF16),
+                pltpu.SemaphoreType.DMA((sems,)),
+                pltpu.SemaphoreType.DMA((sems,)),
+            ],
+            compiler_params=pltpu.CompilerParams(
+                collective_id=0, has_side_effects=True, vmem_limit_bytes=52 * 1024 * 1024
+            ),
+        )(
+            frames, segment_ids.reshape(nt, rows), ln_gain.reshape(1, -1), ln_bias.reshape(1, -1), qkv_weight,
+            out_weight, out_bias.reshape(1, -1), adapter, rms_gain.reshape(1, -1), x_weight, bc_weight, decay,
+            skip_gain.reshape(1, -1),
+        )
+        return encoded, jnp.transpose(mixed, (1, 0, 2)).reshape(toks, xw)
+
+    return per_device
+
+
 def solution(mesh):
     placed = (
         P("tm", "head"),
@@ -192,8 +621,10 @@
         P("tm", "head"),
         P("head"),
     )
+    nt = mesh.shape["tm"]
+    body = fused(nt) if mesh.shape["head"] == 2 and nt % PLANE == 0 else per_device
     return jax.shard_map(
-        per_device,
+        body,
         mesh=mesh,
         in_specs=placed,
         out_specs=(P("tm", "head"), P("tm", "head")),

time: 246 us -> 72.9 us (0.30)
  blocking collectives: 69 us -> 0 us
  waiting for transfers between devices: 65.7 us -> 0 us
  Pallas kernels: 0 us -> 62.8 us
  matrix products: 28.6 us -> 0 us
  other arithmetic: 24.3 us -> 0 us
  local copies, waits for them, and re-layouts: 31 us -> 8.75 us
  between operations: 14.5 us -> 0.65 us
  starting transfers between devices: 10.1 us -> 0 us
    all_gather x1 -> x0, waiting for transfers between devices: 65.7 us -> none  [prefix(): gathered = jax.tree.map(lambda a: lax.all_gather(a, axis), part)]
    all_gather x6 -> x0, blocking collectives: 65.2 us -> none  [the longest x1 24 us: prefix(): gathered = jax.tree.map(lambda a: lax.all_gather(a, axis), part)]
    pallas_call x0 -> x1, Pallas kernels: none -> 62.8 us  [per_device(): pl.pallas_call(functools.partial(fused_kernel, nt), out_shape=(jax.ShapeD...]
    dot_general x12 -> x0, matrix products: 22.5 us -> none  [the longest x1 4.17 us: per_device(): jnp.dot(scaled, x_weight, preferred_element_type=jnp.float32)]
    add x15 -> x0, other arithmetic: 18.7 us -> none  [combine_states(): later[0][:, None, None] * earlier[1] + later[1]]
    mul x15 -> x0, local copies, waits for them, and re-layouts: 10.3 us -> none  [combine_states(): later[0][:, None, None] * earlier[1] + later[1]]
    sub x1 -> x0, matrix products: 6.11 us -> none  [attend(): raised = jnp.exp(scores - peak)]
    all_to_all x1 -> x0, local copies, waits for them, and re-layouts: 5.63 us -> none  [per_device(): lax.all_to_all(adapter, 'head', split_axis=1, concat_axis=0, tiled=True)]
  transfers between devices with their start and end apart: 4 -> 0, of which waited for: 1 -> 0; matrix products, arithmetic and copies ran while one was open for 13% -> 0% of each run, Pallas kernels for 0% -> 0%
where the time goes in v1:
time: 72.9 us; the launch traced here: 72.2 us
  Pallas kernels  62.8 us (86%)
  local copies, waits for them, and re-layouts  8.75 us (12%)
    pallas_call x1, Pallas kernels, per_device(): pl.pallas_call(functools.partial(fused_kernel, nt), out_shape=(jax.ShapeD...  62.8 us
    unnamed x8, local copies, waits for them, and re-layouts  4.23 us

profile of v1, /device:TPU:27, one launch (start us, length us, event | category | flops | bytes accessed | tf_op | source)
XLA Modules:
  0.0 72.2 jit_solution(13071257729241923987)
XLA Ops:
  0.6 0.8 %copy.16.decay = f32[64,20]{1,0:T(8,128)S(1)} copy(f32[64,20]{0,1:T(8,128)} %param.24) | data formatting | bytes 10240 | tf_op args[11]
  1.4 0.7 reshape.25.ids
  2.1 0.7 reshape.29.rms_gain
  2.9 0.7 reshape.26.ln_gain
  3.6 0.7 reshape.27.ln_bias
  4.3 0.7 reshape.28.out_bias
  5.0 0.0 copy-start
  5.0 1.1 %copy-done = bf16[2560,128]{1,0:T(8,128)(2,1)S(1)} copy-done((bf16[2560,128]{1,0:T(8,128)(2,1)S(1)}, bf16[2560,128]{1,0:T(8,128)(2,1)}, u32[]{:S(2)}) %copy-start) | copy-done | bytes 655384
  6.0 0.0 copy-start.1
  6.0 1.0 %copy-done.1 = bf16[256,640]{1,0:T(8,128)(2,1)S(1)} copy-done((bf16[256,640]{1,0:T(8,128)(2,1)S(1)}, bf16[256,640]{1,0:T(8,128)(2,1)}, u32[]{:S(2)}) %copy-start.1) | copy-done | bytes 327704
  7.0 0.0 copy-start.2
  7.0 0.7 copy-done.2
  7.7 62.8 %shard_map.140 = (bf16[256,640]{1,0:T(8,128)(2,1)S(1)}, bf16[4,64,320]{2,1,0:T(8,128)(2,1)S(1)}) custom-call(bf16[256,640]{1,0:T(8,128)(2,1)S(1)} %copy-done.1, s32[16,256]{1,0:T(8,128)S(1)} %reshape.25.ids, f32[1,1280]{1,0:T(1,128)S(1)} %reshape.26.ln_gain, f32[1,1280]{1,0:T(1,128)S(1)} %reshape.27.ln_bias, bf16[3,1280,512]{2,1,0:T(8,128)(2,1)} %qkv_hbm.1, ...), custom_call_target="tpu_custom_call" | custom-call | tf_op jit(solution)/shard_map/pallas_call | solution.py:551
  70.5 0.2 copy.17
  70.7 0.8 %reshape.31 = bf16[64,1280]{1,0:T(8,128)(2,1)} reshape(bf16[64,4,320]{2,1,0:T(4,128)(2,1)S(1)} %copy.17) | data formatting | bytes 327680 | tf_op jit(solution)/shard_map/reshape | solution.py:603
  71.5 0.7 %copy.19 = bf16[256,640]{1,0:T(8,128)(2,1)} copy(bf16[256,640]{1,0:T(8,128)(2,1)S(1)} %get-tuple-element.8) | data formatting | bytes 655360
Async XLA Ops:
  5.0 1.1 %copy-start = (bf16[2560,128]{1,0:T(8,128)(2,1)S(1)}, bf16[2560,128]{1,0:T(8,128)(2,1)}, u32[]{:S(2)}) copy-start(bf16[2560,128]{1,0:T(8,128)(2,1)} %bc_hbm.1) | copy-start | bytes 1966084
  6.0 1.0 %copy-start.1 = (bf16[256,640]{1,0:T(8,128)(2,1)S(1)}, bf16[256,640]{1,0:T(8,128)(2,1)}, u32[]{:S(2)}) copy-start(bf16[256,640]{1,0:T(8,128)(2,1)} %frames.1) | copy-start | bytes 983044
  7.0 0.7 copy-start.2

commit v2 on v1

--- a/solution.py
+++ b/solution.py
@@ -182,7 +182,9 @@
 PLANE = 4
 MESH = pl.DeviceIdType.MESH
 VM = pl.BlockSpec(memory_space=pltpu.VMEM)
-HB = pl.BlockSpec(memory_space=pl.ANY)
+HB = pl.BlockSpec(memory_space=pltpu.HBM)
+S_DECAY, S_K, S_V, S_ATT, S_CP, S_X, S_BC, S_T, S_S1, S_S2, S_Y, S_PART = 1, 4, 6, 8, 12, 13, 16, 19, 20, 21, 22, 25
+PIECES = 5
 F32 = jnp.float32
 BF16 = jnp.bfloat16
 NT = (((1,), (1,)), ((), ()))
@@ -199,26 +201,25 @@
 
 def fused_kernel(
     nt,
-    frames, ids, ln_gain, ln_bias, qkv_hbm, out_hbm, out_bias, ad_hbm, rms_gain, x_hbm, bc_hbm, decay, skip,
+    frames_hbm, ids_hbm, lng_hbm, lnb_hbm, qkv_hbm, out_hbm, ob_hbm, ad_hbm, rms_hbm, x_hbm, bc_hbm, decay_hbm, skip_hbm,
     enc_o, mix_o,
-    wqkv, wout, wad, wx, wbc, wsem,
+    wqkv, wout, wad, wx, wbc, ids, ln_gain, ln_bias, out_bias, rms_gain, skip, wsem,
     fb, nb, qb, kb, vb, mk, acc, mb, lb, att, pf, ps, pr, sc, cp, xin, xq, xb, bcb, db,
-    sm, sb, inc, yacc, yb, yr, send, recv,
+    sm, pm, s1, s2, tp, tn, yacc, yb, yr, send, recv,
 ):
     tm = lax.axis_index("tm")
     hy = lax.axis_index("head")
     z = tm // PLANE
     q = tm % PLANE
     planes = nt // PLANE
-    rows = frames.shape[0]
-    half = frames.shape[1]
-    toks = decay.shape[0]
+    rows = frames_hbm.shape[0]
+    toks = decay_hbm.shape[1]
     span = PLANE * toks
     width = qb.shape[1]
     pairs = width // 128
     qw = xb.shape[2]
     qheads = qw // HDIM
-    heads = decay.shape[1]
+    heads = decay_hbm.shape[0]
 
     loads = [
         pltpu.make_async_copy(src, dst, wsem.at[i])
@@ -231,6 +232,14 @@
                 (ad_hbm, wad),
                 (bc_hbm, wbc),
                 (x_hbm, wx),
+                (frames_hbm, fb.at[hy]),
+                (decay_hbm, db.at[q]),
+                (ids_hbm, ids),
+                (lng_hbm, ln_gain),
+                (lnb_hbm, ln_bias),
+                (ob_hbm, out_bias),
+                (rms_hbm, rms_gain),
+                (skip_hbm, skip),
             ]
         )
     ]
@@ -266,21 +275,27 @@
     def _():
         greet(after)
 
-    for load in loads:
+    for load in loads[7:]:
         load.start()
-    fb[hy] = frames[...]
-    db[q] = decay[...]
+    for load in loads[:7]:
+        load.start()
     pl.semaphore_wait(bar, PLANE + planes - 1 + cross_prev.astype(jnp.int32) + cross_next.astype(jnp.int32))
 
-    c_frames = remote(frames, fb.at[hy], 0, partner)
+    c_frames = remote(frames_hbm, fb.at[hy], 0, partner)
     c_frames.start()
-    c_decay = [remote(decay, db.at[q], k + 1, peer) for k, peer in enumerate(peers)]
+    c_decay = [remote(decay_hbm, db.at[q], S_DECAY + k, peer) for k, peer in enumerate(peers)]
     for c in c_decay:
         c.start()
 
-    own = ids[pl.ds(tm, 1), :].astype(F32)
-    low = jnp.where(tm > 0, ids[pl.ds((tm + nt - 1) % nt, 1), :].astype(F32), -1.0)
-    high = jnp.where(tm < nt - 1, ids[pl.ds((tm + 1) % nt, 1), :].astype(F32), -1.0)
+    for load in loads[7:]:
+        load.wait()
+
+    def id_row(at):
+        return ids[pl.ds(pl.multiple_of(at * rows, rows), rows)].reshape(1, rows).astype(F32)
+
+    own = id_row(tm)
+    low = jnp.where(tm > 0, id_row((tm + nt - 1) % nt), -1.0)
+    high = jnp.where(tm < nt - 1, id_row((tm + 1) % nt), -1.0)
     own_col = jnp.transpose(jnp.broadcast_to(own, (128, rows)))[:, :1]
     for i, row in enumerate((own, low, high)):
         mk[:, i * rows : (i + 1) * rows] = jnp.where(own_col == row, 0.0, -1e30)
@@ -300,7 +315,7 @@
     center = jnp.mean(both, axis=-1, keepdims=True)
     moved = both - center
     spread = jnp.mean(jnp.square(moved), axis=-1, keepdims=True)
-    nb[...] = (moved * lax.rsqrt(spread + EPSILON) * ln_gain[...] + ln_bias[...]).astype(BF16)
+    nb[...] = (moved * lax.rsqrt(spread + EPSILON) * ln_gain[...].reshape(1, -1) + ln_bias[...].reshape(1, -1)).astype(BF16)
 
     def project(which, dst, scale):
         def tile(j, carry):
@@ -336,11 +351,11 @@
 
     loads[0].wait()
     project(1, kb.at[0], None)
-    c_k = halo(kb, 4)
+    c_k = halo(kb, S_K)
     halo_start(c_k)
     loads[1].wait()
     project(2, vb.at[0], None)
-    c_v = halo(vb, 6)
+    c_v = halo(vb, S_V)
     halo_start(c_v)
     loads[2].wait()
     project(0, qb, jnp.asarray(EHEAD_DIM ** (-0.5), BF16))
@@ -369,7 +384,7 @@
 
     def att_copy(p):
         cols = pl.ds(pl.multiple_of(hy * width + p * 128, 128), 128)
-        return remote(att.at[:, cols], att.at[:, cols], 8 + p, partner)
+        return remote(att.at[:, cols], att.at[:, cols], S_ATT + p, partner)
 
     def with_halos(p, carry):
         cols = pl.ds(pl.multiple_of(p * 128, 128), 128)
@@ -396,7 +411,7 @@
         att_copy(p).wait()
 
     loads[3].wait()
-    encoded = (frames[...].astype(F32) + dot(att[...], wout[...]) + out_bias[...]).astype(BF16)
+    encoded = (fb[hy].astype(F32) + dot(att[...], wout[...]) + out_bias[...].reshape(1, -1)).astype(BF16)
     enc_o[...] = encoded
     rr, cc = iota((toks, rows), 0) * 4, iota((toks, rows), 1)
     pool = jnp.where(jnp.logical_and(cc >= rr, cc < rr + 4), 0.25, 0.0).astype(BF16)
@@ -404,20 +419,26 @@
 
     loads[4].wait()
 
+    piece = wad.shape[1] // PIECES
+
+    def part_copy(j):
+        cols = pl.ds(pl.multiple_of(j * piece, piece), piece)
+        return remote(ps.at[:, cols], pr.at[:, cols], S_PART + j, partner)
+
     def adapt(j, carry):
-        cols = pl.ds(pl.multiple_of(j * 256, 256), 256)
+        cols = pl.ds(pl.multiple_of(j * piece, piece), piece)
         part = dot(pooled, wad[:, cols])
         pf[:, cols] = part
         ps[:, cols] = part.astype(BF16)
+        part_copy(j).start()
         return carry
 
-    lax.fori_loop(0, wad.shape[1] // 256, adapt, 0)
-    c_part = remote(ps, pr, 12, partner)
-    c_part.start()
+    lax.fori_loop(0, PIECES, adapt, 0)
 
     for c in c_decay:
         c.wait()
-    dec = db[...].reshape(span, heads)
+    eye = jnp.where(iota((toks, toks), 0) == iota((toks, toks), 1), 1.0, 0.0)
+    dec = jnp.concatenate([dot(eye, db[j], NT, HIGHEST) for j in range(PLANE)], axis=0)
     picked_row = q * qheads
     sel = jnp.where(iota((heads, 128), 0) == picked_row + iota((heads, 128), 1), 1.0, 0.0)
     sel = jnp.where(iota((heads, 128), 1) < qheads, sel, 0.0)
@@ -431,25 +452,32 @@
     growth = dot(jnp.exp(cum), expand, precision=HIGHEST)
     tail = dot(jnp.exp(cum[span - 1 :, :] - cum), expand, precision=HIGHEST)
     drive = dot(1.0 - dec, expand, precision=HIGHEST)
-    skip_wide = dot(jnp.broadcast_to(skip[...], (8, heads)), expand, precision=HIGHEST)[:1, :]
+    skip_wide = dot(jnp.broadcast_to(skip[...].reshape(1, -1), (8, heads)), expand, precision=HIGHEST)[:1, :]
     total = growth[span - 1 :, :]
-    t0 = total.astype(BF16).astype(F32)
-    t1 = (total - t0).astype(BF16).astype(F32)
-    t2 = total - t0 - t1
-    r16 = iota((16, qw), 0)
-    sm[NSTATE:, :] = jnp.where(r16 == 0, t0, jnp.where(r16 == 1, t1, jnp.where(r16 == 2, t2, 0.0))).astype(BF16)
-
-    c_part.wait()
+    tp[...] = jnp.broadcast_to(total, (8, qw))
+    later = {"tm": (tm + PLANE) % nt}
+    latest = {"tm": (tm + 2 * PLANE) % nt}
+    c_t = remote(tp, tn, S_T, later)
+    c_s1 = remote(sm, s1, S_S1, later)
+    c_s2 = remote(sm, s2, S_S2, latest)
+    c_p = remote(pm, s2, S_S2, latest)
+
+    @pl.when(z < planes - 1)
+    def _():
+        c_t.start()
+
+    for j in range(PIECES):
+        part_copy(j).wait()
     proj = pf[...] + pr[...].astype(F32)
     square = jnp.mean(jnp.square(proj), axis=-1, keepdims=True)
-    sc[...] = (proj * lax.rsqrt(square + EPSILON) * rms_gain[...]).astype(BF16)
+    sc[...] = (proj * lax.rsqrt(square + EPSILON) * rms_gain[...].reshape(1, -1)).astype(BF16)
 
     def silu(v):
         return v / (1.0 + jnp.exp(-v))
 
     loads[5].wait()
     cp[hy] = silu(dot(sc[...], wbc[...])).astype(BF16)
-    c_cp = remote(cp.at[hy], cp.at[hy], 13, partner)
+    c_cp = remote(cp.at[hy], cp.at[hy], S_CP, partner)
     c_cp.start()
     loads[6].wait()
 
@@ -458,18 +486,20 @@
         xin[:, cols] = silu(dot(sc[...], wx[:, cols]))
         return carry
 
-    lax.fori_loop(0, wx.shape[1] // 256, drive_in, 0)
+    tiles = wx.shape[1] // 256
+    lax.fori_loop(0, tiles // 2 + 1, drive_in, 0)
+    c_cp.wait()
+    c_bc = [remote(cp, bcb.at[:, q], S_BC + k - 1, peers[k - 1]) for k in range(1, PLANE)]
+    for c in c_bc:
+        c.start()
+    bcb[:, q] = cp[...]
+    lax.fori_loop(tiles // 2 + 1, tiles, drive_in, 0)
     for j in range(PLANE):
         xq[j] = xin[:, j * qw : (j + 1) * qw].astype(BF16)
-    c_x = [remote(xq.at[(q + k) % PLANE], xb.at[q], 13 + k, peers[k - 1]) for k in range(1, PLANE)]
+    c_x = [remote(xq.at[(q + k) % PLANE], xb.at[q], S_X + k - 1, peers[k - 1]) for k in range(1, PLANE)]
     for c in c_x:
         c.start()
     xb[q] = xq[q]
-    c_cp.wait()
-    c_bc = [remote(cp, bcb.at[:, q], 16 + k, peers[k - 1]) for k in range(1, PLANE)]
-    for c in c_bc:
-        c.start()
-    bcb[:, q] = cp[...]
     for c in c_x:
         c.wait()
     for c in c_bc:
@@ -479,15 +509,16 @@
     b_all = bcb[0].reshape(span, NSTATE)
     c_all = bcb[1].reshape(span, NSTATE)
     driven = x_all * drive
-    sm[:NSTATE, :] = dot(b_all, (driven * tail).astype(BF16), TN).astype(BF16)
-
-    def state_copy(dz):
-        return remote(sm, sb.at[z], 19 + dz, {"tm": (tm + dz * PLANE) % nt})
-
-    for dz in range(1, planes):
-        @pl.when(z + dz < planes)
-        def _():
-            state_copy(dz).start()
+    state = dot(b_all, (driven * tail).astype(BF16), TN)
+    sm[...] = state.astype(BF16)
+
+    @pl.when(z < planes - 1)
+    def _():
+        c_s1.start()
+
+    @pl.when(z == 0)
+    def _():
+        c_s2.start()
 
     affinity = dot(c_all, b_all, NT)
     causal = iota((span, span), 0) >= iota((span, span), 1)
@@ -506,32 +537,44 @@
             yacc[:, h * HDIM : (h + 1) * HDIM] = head_out(h, driven[:, h * HDIM : (h + 1) * HDIM])
     yacc[...] = yacc[...] + skip_wide * x_all
 
-    inc[...] = jnp.zeros(inc.shape, F32)
-    for zp in range(planes - 1):
-        @pl.when(zp < z)
-        def _():
-            pltpu.make_async_remote_copy(
-                src_ref=sm, dst_ref=sb.at[zp], send_sem=send.at[19 + z - zp], recv_sem=recv.at[19 + z - zp],
-                device_id=partner, device_id_type=MESH,
-            ).wait_recv()
-            got = sb[zp].astype(F32)
-            fade = got[NSTATE : NSTATE + 1] + got[NSTATE + 1 : NSTATE + 2] + got[NSTATE + 2 : NSTATE + 3]
-            inc[...] = inc[...] * fade + got[:NSTATE]
-
-    y = yacc[...] + growth * dot(c_all, inc[...].astype(BF16))
+    @pl.when(z > 0)
+    def _():
+        c_t.wait_recv()
+        c_s1.wait_recv()
+
+    @pl.when(z == 1)
+    def _():
+        pm[...] = (state + total * s1[...].astype(F32)).astype(BF16)
+        c_p.start()
+
+    @pl.when(z > 1)
+    def _():
+        c_s2.wait_recv()
+        s1[...] = (s1[...].astype(F32) + tn[:1, :] * s2[...].astype(F32)).astype(BF16)
+
+    @pl.when(z == 0)
+    def _():
+        s1[...] = jnp.zeros(s1.shape, BF16)
+
+    y = yacc[...] + growth * dot(c_all, s1[...])
     yb[...] = y.astype(BF16).reshape(PLANE, toks, qw)
-    base = 19 + planes
-    c_y = [remote(yb.at[(q + k) % PLANE], yr.at[q], base + k - 1, peers[k - 1]) for k in range(1, PLANE)]
+    c_y = [remote(yb.at[(q + k) % PLANE], yr.at[q], S_Y + k - 1, peers[k - 1]) for k in range(1, PLANE)]
     for c in c_y:
         c.start()
     yr[q] = yb[q]
-    for dz in range(1, planes):
-        @pl.when(z + dz < planes)
-        def _():
-            state_copy(dz).wait_send()
+    @pl.when(z < planes - 1)
+    def _():
+        c_t.wait_send()
+        c_s1.wait_send()
+
+    @pl.when(z < planes - 2)
+    def _():
+        c_s2.wait_send()
+
     for c in c_y:
         c.wait()
-    mix_o[...] = yr[...]
+    for j in range(PLANE):
+        mix_o[:, j * qw : (j + 1) * qw] = yr[j]
 
 
 def fused(nt):
@@ -546,15 +589,15 @@
         planes = nt // PLANE
         span = PLANE * toks
         pairs = width // 128
-        sems = 19 + planes + PLANE - 1
+        sems = S_PART + PIECES
         v = pltpu.VMEM
         encoded, mixed = pl.pallas_call(
             functools.partial(fused_kernel, nt),
             out_shape=(
                 jax.ShapeDtypeStruct((rows, half), BF16),
-                jax.ShapeDtypeStruct((PLANE, toks, qw), BF16),
+                jax.ShapeDtypeStruct((toks, xw), BF16),
             ),
-            in_specs=[VM, VM, VM, VM, HB, HB, VM, HB, VM, HB, HB, VM, VM],
+            in_specs=[HB] * 13,
             out_specs=(VM, VM),
             scratch_shapes=[
                 v(qkv_weight.shape, BF16),
@@ -562,7 +605,13 @@
                 v(adapter.shape, BF16),
                 v(x_weight.shape, BF16),
                 v(bc_weight.shape, BF16),
-                pltpu.SemaphoreType.DMA((7,)),
+                v(segment_ids.shape, jnp.int32),
+                v(ln_gain.shape, F32),
+                v(ln_bias.shape, F32),
+                v(out_bias.shape, F32),
+                v(rms_gain.shape, F32),
+                v(skip_gain.shape, F32),
+                pltpu.SemaphoreType.DMA((15,)),
                 v((2, rows, half), BF16),
                 v((rows, 2 * half), BF16),
                 v((rows, width), BF16),
@@ -582,10 +631,13 @@
                 v((PLANE, toks, qw), BF16),
                 v((PLANE, toks, qw), BF16),
                 v((2, PLANE, toks, NSTATE), BF16),
-                v((PLANE, toks, heads), F32),
-                v((NSTATE + 16, qw), BF16),
-                v((planes, NSTATE + 16, qw), BF16),
-                v((NSTATE, qw), F32),
+                v((PLANE, heads, toks), F32),
+                v((NSTATE, qw), BF16),
+                v((NSTATE, qw), BF16),
+                v((NSTATE, qw), BF16),
+                v((NSTATE, qw), BF16),
+                v((8, qw), F32),
+                v((8, qw), F32),
                 v((span, qw), F32),
                 v((PLANE, toks, qw), BF16),
                 v((PLANE, toks, qw), BF16),
@@ -596,11 +648,10 @@
                 collective_id=0, has_side_effects=True, vmem_limit_bytes=52 * 1024 * 1024
             ),
         )(
-            frames, segment_ids.reshape(nt, rows), ln_gain.reshape(1, -1), ln_bias.reshape(1, -1), qkv_weight,
-            out_weight, out_bias.reshape(1, -1), adapter, rms_gain.reshape(1, -1), x_weight, bc_weight, decay,
-            skip_gain.reshape(1, -1),
+            frames, segment_ids, ln_gain, ln_bias, qkv_weight, out_weight, out_bias, adapter, rms_gain, x_weight,
+            bc_weight, jnp.transpose(decay), skip_gain,
         )
-        return encoded, jnp.transpose(mixed, (1, 0, 2)).reshape(toks, xw)
+        return encoded, mixed
 
     return per_device
 
@@ -622,7 +673,7 @@
         P("head"),
     )
     nt = mesh.shape["tm"]
-    body = fused(nt) if mesh.shape["head"] == 2 and nt % PLANE == 0 else per_device
+    body = fused(nt) if mesh.shape["head"] == 2 and nt == 4 * PLANE else per_device
     return jax.shard_map(
         body,
         mesh=mesh,

time: 72.9 us -> 69.9 us (0.959)
  Pallas kernels: 62.8 us -> 60.1 us
    reshape x6 -> x0, local copies, waits for them, and re-layouts: 4.37 us -> none  [the longest x1 0.84 us: per_device(): return (encoded, jnp.transpose(mixed, (1, 0, 2)).reshape(toks, xw))]
    unnamed x8 -> x20, local copies, waits for them, and re-layouts: 4.23 us -> 8.31 us
    pallas_call x1, Pallas kernels: 62.8 us -> 60.1 us  [per_device(): pl.pallas_call(functools.partial(fused_kernel, nt), out_shape=(jax.ShapeD...]
where the time goes in v2:
time: 69.9 us; the launch traced here: 69.1 us
  Pallas kernels  60.1 us (86%)
  local copies, waits for them, and re-layouts  8.31 us (12%)
    pallas_call x1, Pallas kernels, per_device(): pl.pallas_call(functools.partial(fused_kernel, nt), out_shape=(jax.ShapeD...  60.1 us
    unnamed x20, local copies, waits for them, and re-layouts  8.31 us

profile of v2, /device:TPU:27, one launch (start us, length us, event | category | flops | bytes accessed | tf_op | source)
XLA Modules:
  0.0 69.1 jit_solution(8012698435636080775)
XLA Ops:
  0.6 0.0 copy-start
  0.6 1.1 %copy-done = bf16[2560,128]{1,0:T(8,128)(2,1)S(1)} copy-done((bf16[2560,128]{1,0:T(8,128)(2,1)S(1)}, bf16[2560,128]{1,0:T(8,128)(2,1)}, u32[]{:S(2)}) %copy-start) | copy-done | bytes 655384
  1.7 0.0 copy-start.1
  1.7 1.0 %copy-done.1 = bf16[256,640]{1,0:T(8,128)(2,1)S(1)} copy-done((bf16[256,640]{1,0:T(8,128)(2,1)S(1)}, bf16[256,640]{1,0:T(8,128)(2,1)}, u32[]{:S(2)}) %copy-start.1) | copy-done | bytes 327704
  2.7 0.0 copy-start.2
  2.7 0.7 %copy-done.2 = s32[4096]{0:T(1024)S(1)} copy-done((s32[4096]{0:T(1024)S(1)}, s32[4096]{0:T(1024)}, u32[]{:S(2)}) %copy-start.2) | copy-done | bytes 16408
  3.4 0.0 copy-start.3
  3.4 0.7 %copy-done.3 = f32[2560]{0:T(1024)S(1)} copy-done((f32[2560]{0:T(1024)S(1)}, f32[2560]{0:T(1024)}, u32[]{:S(2)}) %copy-start.3) | copy-done | bytes 10264
  4.1 0.0 copy-start.4
  4.1 0.7 %copy-done.4 = f32[64,20]{0,1:T(8,128)S(1)} copy-done((f32[64,20]{0,1:T(8,128)S(1)}, f32[64,20]{0,1:T(8,128)}, u32[]{:S(2)}) %copy-start.4) | copy-done | bytes 5144
  4.8 0.0 copy-start.5
  4.8 0.7 %copy-done.5 = f32[1280]{0:T(1024)S(1)} copy-done((f32[1280]{0:T(1024)S(1)}, f32[1280]{0:T(1024)}, u32[]{:S(2)}) %copy-start.5) | copy-done | bytes 5144
  5.5 0.0 copy-start.6
  5.5 0.7 %copy-done.6 = f32[1280]{0:T(1024)S(1)} copy-done((f32[1280]{0:T(1024)S(1)}, f32[1280]{0:T(1024)}, u32[]{:S(2)}) %copy-start.6) | copy-done | bytes 5144
  6.2 0.0 copy-start.7
  6.2 0.7 copy-done.7
  6.9 0.0 copy-start.8
  6.9 0.7 copy-done.8
  7.6 60.1 %shard_map.140 = (bf16[256,640]{1,0:T(8,128)(2,1)S(1)}, bf16[64,1280]{1,0:T(8,128)(2,1)S(1)}) custom-call(bf16[256,640]{1,0:T(8,128)(2,1)S(1)} %copy-done.1, s32[4096]{0:T(1024)S(1)} %copy-done.2, f32[1280]{0:T(1024)S(1)} %copy-done.5, f32[1280]{0:T(1024)S(1)} %copy-done.6, bf16[3,1280,512]{2,1,0:T(8,128)(2,1)} %qkv_hbm.1, bf16[1024,640]{1,0:T(8,128)(2,1)} %out_hbm.1, ...), custom_call_target="tpu_custom_call" | custom-call | tf_op jit(solution)/shard_map/pallas_call | solution.py:594
  67.7 0.7 %copy.17 = bf16[256,640]{1,0:T(8,128)(2,1)} copy(bf16[256,640]{1,0:T(8,128)(2,1)S(1)} %get-tuple-element.4) | data formatting | bytes 655360
  68.4 0.7 copy.18
Async XLA Ops:
  0.6 1.1 %copy-start = (bf16[2560,128]{1,0:T(8,128)(2,1)S(1)}, bf16[2560,128]{1,0:T(8,128)(2,1)}, u32[]{:S(2)}) copy-start(bf16[2560,128]{1,0:T(8,128)(2,1)} %bc_hbm.1) | copy-start | bytes 1966084
  1.7 1.0 %copy-start.1 = (bf16[256,640]{1,0:T(8,128)(2,1)S(1)}, bf16[256,640]{1,0:T(8,128)(2,1)}, u32[]{:S(2)}) copy-start(bf16[256,640]{1,0:T(8,128)(2,1)} %frames_hbm.1) | copy-start | bytes 983044
  2.7 0.7 %copy-start.2 = (s32[4096]{0:T(1024)S(1)}, s32[4096]{0:T(1024)}, u32[]{:S(2)}) copy-start(s32[4096]{0:T(1024)} %ids_hbm.1) | copy-start | bytes 49156
  3.4 0.7 %copy-start.3 = (f32[2560]{0:T(1024)S(1)}, f32[2560]{0:T(1024)}, u32[]{:S(2)}) copy-start(f32[2560]{0:T(1024)} %rms_hbm.1) | copy-start | bytes 30724
  4.1 0.7 %copy-start.4 = (f32[64,20]{0,1:T(8,128)S(1)}, f32[64,20]{0,1:T(8,128)}, u32[]{:S(2)}) copy-start(f32[64,20]{0,1:T(8,128)} %param.24) | copy-start | bytes 15364
  4.8 0.7 %copy-start.5 = (f32[1280]{0:T(1024)S(1)}, f32[1280]{0:T(1024)}, u32[]{:S(2)}) copy-start(f32[1280]{0:T(1024)} %lng_hbm.1) | copy-start | bytes 15364
  5.5 0.7 %copy-start.6 = (f32[1280]{0:T(1024)S(1)}, f32[1280]{0:T(1024)}, u32[]{:S(2)}) copy-start(f32[1280]{0:T(1024)} %lnb_hbm.1) | copy-start | bytes 15364
  6.2 0.7 copy-start.7
  6.9 0.7 copy-start.8

commit v3 on v2

--- a/solution.py
+++ b/solution.py
@@ -185,6 +185,9 @@
 HB = pl.BlockSpec(memory_space=pltpu.HBM)
 S_DECAY, S_K, S_V, S_ATT, S_CP, S_X, S_BC, S_T, S_S1, S_S2, S_Y, S_PART = 1, 4, 6, 8, 12, 13, 16, 19, 20, 21, 22, 25
 PIECES = 5
+S_OFF, S_ON = 30, 32
+CHUNKS = 2
+LIMIT = 63 * 1024 * 1024
 F32 = jnp.float32
 BF16 = jnp.bfloat16
 NT = (((1,), (1,)), ((), ()))
@@ -204,7 +207,7 @@
     frames_hbm, ids_hbm, lng_hbm, lnb_hbm, qkv_hbm, out_hbm, ob_hbm, ad_hbm, rms_hbm, x_hbm, bc_hbm, decay_hbm, skip_hbm,
     enc_o, mix_o,
     wqkv, wout, wad, wx, wbc, ids, ln_gain, ln_bias, out_bias, rms_gain, skip, wsem,
-    fb, nb, qb, kb, vb, mk, acc, mb, lb, att, pf, ps, pr, sc, cp, xin, xq, xb, bcb, db,
+    fb, ob, nb, qb, kb, vb, mk, acc, mb, lb, att, pf, ps, pr, sc, cp, xin, xq, xb, bcb, db,
     sm, pm, s1, s2, tp, tn, yacc, yb, yr, send, recv,
 ):
     tm = lax.axis_index("tm")
@@ -252,8 +255,12 @@
 
     partner = {"head": 1 - hy}
     peers = [{"tm": z * PLANE + (q + k) % PLANE} for k in range(1, PLANE)]
-    prev = {"tm": (tm + nt - 1) % nt}
-    after = {"tm": (tm + 1) % nt}
+    side = tm % 2
+    off_at = (tm + nt - 1 + 2 * side) % nt
+    on_at = tm + 1 - 2 * side
+    off = {"tm": off_at}
+    on = {"tm": on_at}
+    has_off = jnp.logical_and(tm > 0, tm < nt - 1)
     bar = pltpu.get_barrier_semaphore()
 
     def greet(device):
@@ -264,25 +271,41 @@
         greet(peer)
     for dz in range(1, planes):
         greet({"tm": (tm + dz * PLANE) % nt})
-    cross_prev = jnp.logical_and(q == 0, tm > 0)
-    cross_next = jnp.logical_and(q == PLANE - 1, tm < nt - 1)
-
-    @pl.when(cross_prev)
-    def _():
-        greet(prev)
-
-    @pl.when(cross_next)
-    def _():
-        greet(after)
+    far = jnp.logical_and(has_off, jnp.logical_or(q == 0, q == PLANE - 1))
+
+    @pl.when(far)
+    def _():
+        greet(off)
 
     for load in loads[7:]:
         load.start()
     for load in loads[:7]:
         load.start()
-    pl.semaphore_wait(bar, PLANE + planes - 1 + cross_prev.astype(jnp.int32) + cross_next.astype(jnp.int32))
+    pl.semaphore_wait(bar, PLANE + planes - 1 + far.astype(jnp.int32))
 
     c_frames = remote(frames_hbm, fb.at[hy], 0, partner)
     c_frames.start()
+    step = rows // CHUNKS
+
+    def off_copy(i):
+        part = pl.ds(i * step, step)
+        return remote(frames_hbm.at[part, :], ob.at[hy, part, :], S_OFF + i, off)
+
+    def on_copy(i):
+        part = pl.ds(i * step, step)
+        return remote(ob.at[hy, part, :], ob.at[hy, part, :], S_ON + i, partner)
+
+    def hand_on(i):
+        @pl.when(has_off)
+        def _():
+            off_copy(i).wait_recv()
+            on_copy(i).start()
+
+    @pl.when(has_off)
+    def _():
+        for i in range(CHUNKS):
+            off_copy(i).start()
+
     c_decay = [remote(decay_hbm, db.at[q], S_DECAY + k, peer) for k, peer in enumerate(peers)]
     for c in c_decay:
         c.start()
@@ -294,28 +317,22 @@
         return ids[pl.ds(pl.multiple_of(at * rows, rows), rows)].reshape(1, rows).astype(F32)
 
     own = id_row(tm)
-    low = jnp.where(tm > 0, id_row((tm + nt - 1) % nt), -1.0)
-    high = jnp.where(tm < nt - 1, id_row((tm + 1) % nt), -1.0)
+    beside = id_row(on_at)
+    beyond = jnp.where(has_off, id_row(off_at), -1.0)
     own_col = jnp.transpose(jnp.broadcast_to(own, (128, rows)))[:, :1]
-    for i, row in enumerate((own, low, high)):
+    for i, row in enumerate((own, beside, beyond)):
         mk[:, i * rows : (i + 1) * rows] = jnp.where(own_col == row, 0.0, -1e30)
 
-    @pl.when(tm == 0)
-    def _():
-        kb[1] = jnp.zeros((rows, width), BF16)
-        vb[1] = jnp.zeros((rows, width), BF16)
-
-    @pl.when(tm == nt - 1)
-    def _():
-        kb[2] = jnp.zeros((rows, width), BF16)
-        vb[2] = jnp.zeros((rows, width), BF16)
+    def normalize(buf):
+        both = jnp.concatenate([buf[0], buf[1]], axis=1).astype(F32)
+        center = jnp.mean(both, axis=-1, keepdims=True)
+        moved = both - center
+        spread = jnp.mean(jnp.square(moved), axis=-1, keepdims=True)
+        scale = ln_gain[...].reshape(1, -1)
+        nb[...] = (moved * lax.rsqrt(spread + EPSILON) * scale + ln_bias[...].reshape(1, -1)).astype(BF16)
 
     c_frames.wait()
-    both = jnp.concatenate([fb[0], fb[1]], axis=1).astype(F32)
-    center = jnp.mean(both, axis=-1, keepdims=True)
-    moved = both - center
-    spread = jnp.mean(jnp.square(moved), axis=-1, keepdims=True)
-    nb[...] = (moved * lax.rsqrt(spread + EPSILON) * ln_gain[...].reshape(1, -1) + ln_bias[...].reshape(1, -1)).astype(BF16)
+    normalize(fb)
 
     def project(which, dst, scale):
         def tile(j, carry):
@@ -326,37 +343,16 @@
 
         lax.fori_loop(0, width // 256, tile, 0)
 
-    def halo(buf, sem):
-        return (remote(buf.at[0], buf.at[1], sem, after), remote(buf.at[0], buf.at[2], sem + 1, prev))
-
-    def halo_start(pair):
-        @pl.when(tm < nt - 1)
-        def _():
-            pair[0].start()
-
-        @pl.when(tm > 0)
-        def _():
-            pair[1].start()
-
-    def halo_wait(pair):
-        @pl.when(tm > 0)
-        def _():
-            pair[0].wait_recv()
-            pair[1].wait_send()
-
-        @pl.when(tm < nt - 1)
-        def _():
-            pair[0].wait_send()
-            pair[1].wait_recv()
-
     loads[0].wait()
     project(1, kb.at[0], None)
-    c_k = halo(kb, S_K)
-    halo_start(c_k)
+    c_k = remote(kb.at[0], kb.at[1], S_K, on)
+    c_k.start()
+    hand_on(0)
     loads[1].wait()
     project(2, vb.at[0], None)
-    c_v = halo(vb, S_V)
-    halo_start(c_v)
+    c_v = remote(vb.at[0], vb.at[1], S_V, on)
+    c_v.start()
+    hand_on(1)
     loads[2].wait()
     project(0, qb, jnp.asarray(EHEAD_DIM ** (-0.5), BF16))
 
@@ -364,12 +360,14 @@
     is_low = lane < EHEAD_DIM
     sides = (jnp.where(is_low, 1.0, 0.0).astype(BF16), jnp.where(is_low, 0.0, 1.0).astype(BF16))
 
-    def within_own(p, carry):
+    def within_chip(p, carry):
         cols = pl.ds(pl.multiple_of(p * 128, 128), 128)
-        qp, kp, vp = qb[:, cols], kb[0, :, cols], vb[0, :, cols]
+        qp = qb[:, cols]
+        kp = kb[:2, :, cols].reshape(2 * rows, 128)
+        vp = vb[:2, :, cols].reshape(2 * rows, 128)
         got = []
         for side in sides:
-            s = dot(qp * side, kp, NT) + mk[:, :rows]
+            s = dot(qp * side, kp, NT) + mk[:, : 2 * rows]
             m = jnp.max(s, axis=-1, keepdims=True)
             e = jnp.exp(s - m)
             got.append((dot(e.astype(BF16), vp), m, jnp.sum(e, axis=-1, keepdims=True)))
@@ -378,23 +376,36 @@
         lb[p] = jnp.where(is_low, got[0][2], got[1][2])
         return carry
 
-    lax.fori_loop(0, pairs, within_own, 0)
-    halo_wait(c_k)
-    halo_wait(c_v)
+    c_k.wait()
+    c_v.wait()
+    lax.fori_loop(0, pairs, within_chip, 0)
+
+    @pl.when(has_off)
+    def _():
+        for i in range(CHUNKS):
+            on_copy(i).wait()
+            off_copy(i).wait_send()
+        normalize(ob)
+        project(1, kb.at[2], None)
+        project(2, vb.at[2], None)
+
+    @pl.when(jnp.logical_not(has_off))
+    def _():
+        kb[2] = jnp.zeros((rows, width), BF16)
+        vb[2] = jnp.zeros((rows, width), BF16)
 
     def att_copy(p):
         cols = pl.ds(pl.multiple_of(hy * width + p * 128, 128), 128)
         return remote(att.at[:, cols], att.at[:, cols], S_ATT + p, partner)
 
-    def with_halos(p, carry):
+    def beyond_chip(p, carry):
         cols = pl.ds(pl.multiple_of(p * 128, 128), 128)
         qp = qb[:, cols]
-        kp = kb[1:3, :, cols].reshape(2 * rows, 128)
-        vp = vb[1:3, :, cols].reshape(2 * rows, 128)
+        kp, vp = kb[2, :, cols], vb[2, :, cols]
         old_m, old_l = mb[p], lb[p]
         got = []
         for i, side in enumerate(sides):
-            s = dot(qp * side, kp, NT) + mk[:, rows:]
+            s = dot(qp * side, kp, NT) + mk[:, 2 * rows :]
             m1 = old_m[:, i * EHEAD_DIM : i * EHEAD_DIM + 1]
             m = jnp.maximum(jnp.max(s, axis=-1, keepdims=True), m1)
             e = jnp.exp(s - m)
@@ -406,7 +417,7 @@
         att_copy(p).start()
         return carry
 
-    lax.fori_loop(0, pairs, with_halos, 0)
+    lax.fori_loop(0, pairs, beyond_chip, 0)
     for p in range(pairs):
         att_copy(p).wait()
 
@@ -589,7 +600,7 @@
         planes = nt // PLANE
         span = PLANE * toks
         pairs = width // 128
-        sems = S_PART + PIECES
+        sems = S_ON + CHUNKS
         v = pltpu.VMEM
         encoded, mixed = pl.pallas_call(
             functools.partial(fused_kernel, nt),
@@ -612,6 +623,7 @@
                 v(rms_gain.shape, F32),
                 v(skip_gain.shape, F32),
                 pltpu.SemaphoreType.DMA((15,)),
+                v((2, rows, half), BF16),
                 v((2, rows, half), BF16),
                 v((rows, 2 * half), BF16),
                 v((rows, width), BF16),
@@ -645,7 +657,7 @@
                 pltpu.SemaphoreType.DMA((sems,)),
             ],
             compiler_params=pltpu.CompilerParams(
-                collective_id=0, has_side_effects=True, vmem_limit_bytes=52 * 1024 * 1024
+                collective_id=0, has_side_effects=True, vmem_limit_bytes=LIMIT
             ),
         )(
             frames, segment_ids, ln_gain, ln_bias, qkv_weight, out_weight, out_bias, adapter, rms_gain, x_weight,

time: 69.9 us -> 63.9 us (0.914)
  local copies, waits for them, and re-layouts: 8.31 us -> 3.32 us
    unnamed x20 -> x2, local copies, waits for them, and re-layouts: 8.31 us -> 3.32 us
where the time goes in v3:
time: 63.9 us; the launch traced here: 63.8 us
  Pallas kernels  59.8 us (94%)
  local copies, waits for them, and re-layouts  3.32 us (5%)
  between operations  0.64 us (1%)
    pallas_call x1, Pallas kernels, per_device(): pl.pallas_call(functools.partial(fused_kernel, nt), out_shape=(jax.ShapeD...  59.8 us
    unnamed x2, local copies, waits for them, and re-layouts  3.32 us

profile of v3, /device:TPU:27, one launch (start us, length us, event | category | flops | bytes accessed | tf_op | source)
XLA Modules:
  0.0 63.8 jit_solution(3899457603384975349)
XLA Ops:
  0.6 59.8 %shard_map.140 = (bf16[256,640]{1,0:T(8,128)(2,1)}, bf16[64,1280]{1,0:T(8,128)(2,1)}) custom-call(bf16[256,640]{1,0:T(8,128)(2,1)} %frames_hbm.1, s32[4096]{0:T(1024)} %ids_hbm.1, f32[1280]{0:T(1024)} %lng_hbm.1, f32[1280]{0:T(1024)} %lnb_hbm.1, bf16[3,1280,512]{2,1,0:T(8,128)(2,1)} %qkv_hbm.1, bf16[1024,640]{1,0:T(8,128)(2,1)} %out_hbm.1, f32[640]{0:T(1024)} %ob_hbm.1, ...), custom_call_target="tpu_custom_call" | custom-call | tf_op jit(solution)/shard_map/pallas_call | solution.py:605
  60.5 1.7 %copy.17 = bf16[256,640]{1,0:T(8,128)(2,1)} copy(bf16[256,640]{1,0:T(8,128)(2,1)} %get-tuple-element.4) | data formatting | bytes 655360
  62.2 1.6 %copy.18 = bf16[64,1280]{1,0:T(8,128)(2,1)} copy(bf16[64,1280]{1,0:T(8,128)(2,1)} %get-tuple-element.5) | data formatting | bytes 327680

commit v4 on v3

--- a/solution.py
+++ b/solution.py
@@ -208,7 +208,7 @@
     enc_o, mix_o,
     wqkv, wout, wad, wx, wbc, ids, ln_gain, ln_bias, out_bias, rms_gain, skip, wsem,
     fb, ob, nb, qb, kb, vb, mk, acc, mb, lb, att, pf, ps, pr, sc, cp, xin, xq, xb, bcb, db,
-    sm, pm, s1, s2, tp, tn, yacc, yb, yr, send, recv,
+    sm, pm, s1, s2, tp, tn, wgt, dx, skx, yacc, yb, yr, send, recv,
 ):
     tm = lax.axis_index("tm")
     hy = lax.axis_index("head")
@@ -331,6 +331,43 @@
         scale = ln_gain[...].reshape(1, -1)
         nb[...] = (moved * lax.rsqrt(spread + EPSILON) * scale + ln_bias[...].reshape(1, -1)).astype(BF16)
 
+    for c in c_decay:
+        c.wait()
+    eye = jnp.where(iota((toks, toks), 0) == iota((toks, toks), 1), 1.0, 0.0)
+    dec = jnp.concatenate([dot(eye, db[j], NT, HIGHEST) for j in range(PLANE)], axis=0)
+    picked_row = q * qheads
+    sel = jnp.where(iota((heads, 128), 0) == picked_row + iota((heads, 128), 1), 1.0, 0.0)
+    sel = jnp.where(iota((heads, 128), 1) < qheads, sel, 0.0)
+    first = (iota((heads, qw), 0) - picked_row) * HDIM
+    wide = iota((heads, qw), 1)
+    expand = jnp.where(jnp.logical_and(wide >= first, wide < first + HDIM), 1.0, 0.0)
+    tri = jnp.where(iota((span, span), 0) >= iota((span, span), 1), 1.0, 0.0)
+    cum = dot(tri, jnp.log(jnp.maximum(dec, 1e-37)), precision=HIGHEST)
+    cum_col = dot(cum, sel, precision=HIGHEST)
+    cum_row = jnp.transpose(cum_col)
+    growth = dot(jnp.exp(cum), expand, precision=HIGHEST)
+    drive = dot(1.0 - dec, expand, precision=HIGHEST)
+    dx[0] = growth
+    dx[1] = dot(jnp.exp(cum[span - 1 :, :] - cum) * (1.0 - dec), expand, precision=HIGHEST)
+    dx[2] = drive
+    skx[...] = dot(jnp.broadcast_to(skip[...].reshape(1, -1), (8, heads)), expand, precision=HIGHEST)
+    causal = iota((span, span), 0) >= iota((span, span), 1)
+    for h in range(qheads):
+        gap = cum_col[:, h : h + 1] - cum_row[h : h + 1, :]
+        wgt[h] = jnp.exp(jnp.where(causal, gap, -1e30))
+    total = growth[span - 1 :, :]
+    tp[...] = jnp.broadcast_to(total, (8, qw))
+    later = {"tm": (tm + PLANE) % nt}
+    latest = {"tm": (tm + 2 * PLANE) % nt}
+    c_t = remote(tp, tn, S_T, later)
+    c_s1 = remote(sm, s1, S_S1, later)
+    c_s2 = remote(sm, s2, S_S2, latest)
+    c_p = remote(pm, s2, S_S2, latest)
+
+    @pl.when(z < planes - 1)
+    def _():
+        c_t.start()
+
     c_frames.wait()
     normalize(fb)
 
@@ -446,37 +483,6 @@
 
     lax.fori_loop(0, PIECES, adapt, 0)
 
-    for c in c_decay:
-        c.wait()
-    eye = jnp.where(iota((toks, toks), 0) == iota((toks, toks), 1), 1.0, 0.0)
-    dec = jnp.concatenate([dot(eye, db[j], NT, HIGHEST) for j in range(PLANE)], axis=0)
-    picked_row = q * qheads
-    sel = jnp.where(iota((heads, 128), 0) == picked_row + iota((heads, 128), 1), 1.0, 0.0)
-    sel = jnp.where(iota((heads, 128), 1) < qheads, sel, 0.0)
-    first = (iota((heads, qw), 0) - picked_row) * HDIM
-    wide = iota((heads, qw), 1)
-    expand = jnp.where(jnp.logical_and(wide >= first, wide < first + HDIM), 1.0, 0.0)
-    tri = jnp.where(iota((span, span), 0) >= iota((span, span), 1), 1.0, 0.0)
-    cum = dot(tri, jnp.log(jnp.maximum(dec, 1e-37)), precision=HIGHEST)
-    cum_col = dot(cum, sel, precision=HIGHEST)
-    cum_row = jnp.transpose(cum_col)
-    growth = dot(jnp.exp(cum), expand, precision=HIGHEST)
-    tail = dot(jnp.exp(cum[span - 1 :, :] - cum), expand, precision=HIGHEST)
-    drive = dot(1.0 - dec, expand, precision=HIGHEST)
-    skip_wide = dot(jnp.broadcast_to(skip[...].reshape(1, -1), (8, heads)), expand, precision=HIGHEST)[:1, :]
-    total = growth[span - 1 :, :]
-    tp[...] = jnp.broadcast_to(total, (8, qw))
-    later = {"tm": (tm + PLANE) % nt}
-    latest = {"tm": (tm + 2 * PLANE) % nt}
-    c_t = remote(tp, tn, S_T, later)
-    c_s1 = remote(sm, s1, S_S1, later)
-    c_s2 = remote(sm, s2, S_S2, latest)
-    c_p = remote(pm, s2, S_S2, latest)
-
-    @pl.when(z < planes - 1)
-    def _():
-        c_t.start()
-
     for j in range(PIECES):
         part_copy(j).wait()
     proj = pf[...] + pr[...].astype(F32)
@@ -519,8 +525,7 @@
     x_all = xb[...].reshape(span, qw).astype(F32)
     b_all = bcb[0].reshape(span, NSTATE)
     c_all = bcb[1].reshape(span, NSTATE)
-    driven = x_all * drive
-    state = dot(b_all, (driven * tail).astype(BF16), TN)
+    state = dot(b_all, (x_all * dx[1]).astype(BF16), TN)
     sm[...] = state.astype(BF16)
 
     @pl.when(z < planes - 1)
@@ -532,13 +537,10 @@
         c_s2.start()
 
     affinity = dot(c_all, b_all, NT)
-    causal = iota((span, span), 0) >= iota((span, span), 1)
-    driven = driven.astype(BF16)
+    driven = (x_all * dx[2]).astype(BF16)
 
     def head_out(h, cols):
-        gap = cum_col[:, h : h + 1] - cum_row[h : h + 1, :]
-        mixing = affinity * jnp.exp(jnp.where(causal, gap, -1e30))
-        return dot(mixing.astype(BF16), cols)
+        return dot((affinity * wgt[h]).astype(BF16), cols)
 
     for h in range(0, qheads, 2):
         if h + 1 < qheads:
@@ -546,7 +548,7 @@
             yacc[:, h * HDIM : (h + 2) * HDIM] = jnp.where(is_low, head_out(h, cols), head_out(h + 1, cols))
         else:
             yacc[:, h * HDIM : (h + 1) * HDIM] = head_out(h, driven[:, h * HDIM : (h + 1) * HDIM])
-    yacc[...] = yacc[...] + skip_wide * x_all
+    yacc[...] = yacc[...] + skx[:1, :] * x_all
 
     @pl.when(z > 0)
     def _():
@@ -555,7 +557,7 @@
 
     @pl.when(z == 1)
     def _():
-        pm[...] = (state + total * s1[...].astype(F32)).astype(BF16)
+        pm[...] = (sm[...].astype(F32) + tp[:1, :] * s1[...].astype(F32)).astype(BF16)
         c_p.start()
 
     @pl.when(z > 1)
@@ -567,7 +569,7 @@
     def _():
         s1[...] = jnp.zeros(s1.shape, BF16)
 
-    y = yacc[...] + growth * dot(c_all, s1[...])
+    y = yacc[...] + dx[0] * dot(c_all, s1[...])
     yb[...] = y.astype(BF16).reshape(PLANE, toks, qw)
     c_y = [remote(yb.at[(q + k) % PLANE], yr.at[q], S_Y + k - 1, peers[k - 1]) for k in range(1, PLANE)]
     for c in c_y:
@@ -586,6 +588,14 @@
         c.wait()
     for j in range(PLANE):
         mix_o[:, j * qw : (j + 1) * qw] = yr[j]
+
+
+def place_kernel(a, b, a_out, b_out, sem):
+    moves = [pltpu.make_async_copy(a, a_out, sem.at[0]), pltpu.make_async_copy(b, b_out, sem.at[1])]
+    for move in moves:
+        move.start()
+    for move in moves:
+        move.wait()
 
 
 def fused(nt):
@@ -650,6 +660,9 @@
                 v((NSTATE, qw), BF16),
                 v((8, qw), F32),
                 v((8, qw), F32),
+                v((qw // HDIM, span, span), F32),
+                v((3, span, qw), F32),
+                v((8, qw), F32),
                 v((span, qw), F32),
                 v((PLANE, toks, qw), BF16),
                 v((PLANE, toks, qw), BF16),
@@ -663,7 +676,13 @@
             frames, segment_ids, ln_gain, ln_bias, qkv_weight, out_weight, out_bias, adapter, rms_gain, x_weight,
             bc_weight, jnp.transpose(decay), skip_gain,
         )
-        return encoded, mixed
+        return pl.pallas_call(
+            place_kernel,
+            out_shape=(jax.ShapeDtypeStruct(encoded.shape, BF16), jax.ShapeDtypeStruct(mixed.shape, BF16)),
+            in_specs=[HB, HB],
+            out_specs=(HB, HB),
+            scratch_shapes=[pltpu.SemaphoreType.DMA((2,))],
+        )(encoded, mixed)
 
     return per_device
 

time: 63.9 us -> 81.5 us (1.28)
  Pallas kernels: 59.8 us -> 80.8 us
  local copies, waits for them, and re-layouts: 3.32 us -> 0 us
    pallas_call x0 -> x1, Pallas kernels: none -> 16 us  [per_device(): pl.pallas_call(place_kernel, out_shape=(jax.ShapeDtypeStruct(encoded.shap...]
    pallas_call x1, Pallas kernels: 59.8 us -> 64.7 us  [per_device(): pl.pallas_call(functools.partial(fused_kernel, nt), out_shape=(jax.ShapeD...]
    unnamed x2 -> x0, local copies, waits for them, and re-layouts: 3.32 us -> none
where the time goes in v4:
time: 81.5 us; the launch traced here: 81.4 us
  Pallas kernels  80.8 us (99%)
    pallas_call x1, Pallas kernels, per_device(): pl.pallas_call(functools.partial(fused_kernel, nt), out_shape=(jax.ShapeD...  64.7 us
    pallas_call x1, Pallas kernels, per_device(): pl.pallas_call(place_kernel, out_shape=(jax.ShapeDtypeStruct(encoded.shap...  16 us

profile of v4, /device:TPU:27, one launch (start us, length us, event | category | flops | bytes accessed | tf_op | source)
XLA Modules:
  0.0 81.4 jit_solution(11342571639300359480)
XLA Ops:
  0.6 64.7 %shard_map.140 = (bf16[256,640]{1,0:T(8,128)(2,1)}, bf16[64,1280]{1,0:T(8,128)(2,1)}) custom-call(bf16[256,640]{1,0:T(8,128)(2,1)} %frames_hbm.1, s32[4096]{0:T(1024)} %ids_hbm.1, f32[1280]{0:T(1024)} %lng_hbm.1, f32[1280]{0:T(1024)} %lnb_hbm.1, bf16[3,1280,512]{2,1,0:T(8,128)(2,1)} %qkv_hbm.1, bf16[1024,640]{1,0:T(8,128)(2,1)} %out_hbm.1, f32[640]{0:T(1024)} %ob_hbm.1, ...), custom_call_target="tpu_custom_call" | custom-call | tf_op jit(solution)/shard_map/pallas_call | solution.py:615
  65.4 16.0 %shard_map.141 = (bf16[256,640]{1,0:T(8,128)(2,1)}, bf16[64,1280]{1,0:T(8,128)(2,1)}) custom-call(bf16[256,640]{1,0:T(8,128)(2,1)} %get-tuple-element.4.a, bf16[64,1280]{1,0:T(8,128)(2,1)} %get-tuple-element.5.b), custom_call_target="tpu_custom_call" | custom-call | tf_op jit(solution)/shard_map/pallas_call | solution.py:679

commit v5 on v4

--- a/solution.py
+++ b/solution.py
@@ -331,31 +331,54 @@
         scale = ln_gain[...].reshape(1, -1)
         nb[...] = (moved * lax.rsqrt(spread + EPSILON) * scale + ln_bias[...].reshape(1, -1)).astype(BF16)
 
+    is_low = iota((1, 128), 1) < EHEAD_DIM
+
     for c in c_decay:
         c.wait()
-    eye = jnp.where(iota((toks, toks), 0) == iota((toks, toks), 1), 1.0, 0.0)
-    dec = jnp.concatenate([dot(eye, db[j], NT, HIGHEST) for j in range(PLANE)], axis=0)
-    picked_row = q * qheads
-    sel = jnp.where(iota((heads, 128), 0) == picked_row + iota((heads, 128), 1), 1.0, 0.0)
-    sel = jnp.where(iota((heads, 128), 1) < qheads, sel, 0.0)
-    first = (iota((heads, qw), 0) - picked_row) * HDIM
-    wide = iota((heads, qw), 1)
-    expand = jnp.where(jnp.logical_and(wide >= first, wide < first + HDIM), 1.0, 0.0)
-    tri = jnp.where(iota((span, span), 0) >= iota((span, span), 1), 1.0, 0.0)
-    cum = dot(tri, jnp.log(jnp.maximum(dec, 1e-37)), precision=HIGHEST)
-    cum_col = dot(cum, sel, precision=HIGHEST)
-    cum_row = jnp.transpose(cum_col)
-    growth = dot(jnp.exp(cum), expand, precision=HIGHEST)
-    drive = dot(1.0 - dec, expand, precision=HIGHEST)
-    dx[0] = growth
-    dx[1] = dot(jnp.exp(cum[span - 1 :, :] - cum) * (1.0 - dec), expand, precision=HIGHEST)
-    dx[2] = drive
-    skx[...] = dot(jnp.broadcast_to(skip[...].reshape(1, -1), (8, heads)), expand, precision=HIGHEST)
+    blocks = []
+    for j in range(PLANE):
+        block = db[j]
+        mine = block[:qheads, :]
+        for i in range(1, PLANE):
+            mine = jnp.where(q == i, block[i * qheads : (i + 1) * qheads, :], mine)
+        blocks.append(mine)
+    dec_row = jnp.concatenate(blocks, axis=1)
+    dec_row = jnp.concatenate([dec_row, jnp.ones((8 - qheads, span), F32)], axis=0)
+    logs = jnp.log(jnp.maximum(dec_row, 1e-37))
+    l0 = logs.astype(BF16).astype(F32)
+    l1 = (logs - l0).astype(BF16).astype(F32)
+    l2 = logs - l0 - l1
+    upto = jnp.where(iota((span, span), 0) <= iota((span, span), 1), 1.0, 0.0).astype(BF16)
+    summed = dot(jnp.concatenate([l0, l1, l2, jnp.zeros((8, span), F32)], axis=0).astype(BF16), upto)
+    cum_row = summed[:8] + summed[8:16] + summed[16:24]
+    cols = jnp.transpose(jnp.concatenate([cum_row, dec_row, jnp.zeros((112, span), F32)], axis=0))
+    cum_col = cols[:, :8]
+    rest = 1.0 - cols[:, 8:16]
+    grow = jnp.exp(cum_col)
+    tail = jnp.exp(cum_col[span - 1 :, :] - cum_col) * rest
+
+    def widen(narrow, dst):
+        for h in range(0, qheads, 2):
+            first = jnp.broadcast_to(narrow[:, h : h + 1], (narrow.shape[0], 128))
+            if h + 1 < qheads:
+                second = jnp.broadcast_to(narrow[:, h + 1 : h + 2], (narrow.shape[0], 128))
+                dst[:, h * HDIM : (h + 2) * HDIM] = jnp.where(is_low, first, second)
+            else:
+                dst[:, h * HDIM : (h + 1) * HDIM] = first[:, :HDIM]
+
+    widen(grow, dx.at[0])
+    widen(tail, dx.at[1])
+    widen(rest, dx.at[2])
+    gains = skip[...].reshape(1, -1)
+    own_gain = gains[:, :qheads]
+    for i in range(1, PLANE):
+        own_gain = jnp.where(q == i, gains[:, i * qheads : (i + 1) * qheads], own_gain)
+    widen(jnp.broadcast_to(own_gain, (8, qheads)), skx)
     causal = iota((span, span), 0) >= iota((span, span), 1)
     for h in range(qheads):
         gap = cum_col[:, h : h + 1] - cum_row[h : h + 1, :]
         wgt[h] = jnp.exp(jnp.where(causal, gap, -1e30))
-    total = growth[span - 1 :, :]
+    total = dx[0, span - 1 :, :]
     tp[...] = jnp.broadcast_to(total, (8, qw))
     later = {"tm": (tm + PLANE) % nt}
     latest = {"tm": (tm + 2 * PLANE) % nt}
@@ -393,8 +416,6 @@
     loads[2].wait()
     project(0, qb, jnp.asarray(EHEAD_DIM ** (-0.5), BF16))
 
-    lane = iota((1, 128), 1)
-    is_low = lane < EHEAD_DIM
     sides = (jnp.where(is_low, 1.0, 0.0).astype(BF16), jnp.where(is_low, 0.0, 1.0).astype(BF16))
 
     def within_chip(p, carry):
@@ -590,12 +611,9 @@
         mix_o[:, j * qw : (j + 1) * qw] = yr[j]
 
 
-def place_kernel(a, b, a_out, b_out, sem):
-    moves = [pltpu.make_async_copy(a, a_out, sem.at[0]), pltpu.make_async_copy(b, b_out, sem.at[1])]
-    for move in moves:
-        move.start()
-    for move in moves:
-        move.wait()
+def place_kernel(a, b, a_out, b_out):
+    a_out[...] = a[...]
+    b_out[...] = b[...]
 
 
 def fused(nt):
@@ -679,9 +697,8 @@
         return pl.pallas_call(
             place_kernel,
             out_shape=(jax.ShapeDtypeStruct(encoded.shape, BF16), jax.ShapeDtypeStruct(mixed.shape, BF16)),
-            in_specs=[HB, HB],
-            out_specs=(HB, HB),
-            scratch_shapes=[pltpu.SemaphoreType.DMA((2,))],
+            in_specs=[VM, VM],
+            out_specs=(VM, VM),
         )(encoded, mixed)
 
     return per_device

time: 81.5 us -> 66.8 us (0.82)
  Pallas kernels: 80.8 us -> 66 us
    pallas_call x1, Pallas kernels: 16 us -> 1.82 us  [per_device(): pl.pallas_call(place_kernel, out_shape=(jax.ShapeDtypeStruct(encoded.shap...]
where the time goes in v5:
time: 66.8 us; the launch traced here: 66.7 us
  Pallas kernels  66 us (99%)
    pallas_call x1, Pallas kernels, per_device(): pl.pallas_call(functools.partial(fused_kernel, nt), out_shape=(jax.ShapeD...  64.2 us
    pallas_call x1, Pallas kernels, per_device(): pl.pallas_call(place_kernel, out_shape=(jax.ShapeDtypeStruct(encoded.shap...  1.82 us

profile of v5, /device:TPU:27, one launch (start us, length us, event | category | flops | bytes accessed | tf_op | source)
XLA Modules:
  0.0 66.7 jit_solution(4470533050448853298)
XLA Ops:
  0.6 64.2 %shard_map.140 = (bf16[256,640]{1,0:T(8,128)(2,1)}, bf16[64,1280]{1,0:T(8,128)(2,1)}) custom-call(bf16[256,640]{1,0:T(8,128)(2,1)} %frames_hbm.1, s32[4096]{0:T(1024)} %ids_hbm.1, f32[1280]{0:T(1024)} %lng_hbm.1, f32[1280]{0:T(1024)} %lnb_hbm.1, bf16[3,1280,512]{2,1,0:T(8,128)(2,1)} %qkv_hbm.1, bf16[1024,640]{1,0:T(8,128)(2,1)} %out_hbm.1, f32[640]{0:T(1024)} %ob_hbm.1, ...), custom_call_target="tpu_custom_call" | custom-call | tf_op jit(solution)/shard_map/pallas_call | solution.py:633
  64.9 1.8 %shard_map.141 = (bf16[256,640]{1,0:T(8,128)(2,1)}, bf16[64,1280]{1,0:T(8,128)(2,1)}) custom-call(bf16[256,640]{1,0:T(8,128)(2,1)} %get-tuple-element.4.a, bf16[64,1280]{1,0:T(8,128)(2,1)} %get-tuple-element.5.b), custom_call_target="tpu_custom_call" | custom-call | tf_op jit(solution)/shard_map/pallas_call | solution.py:697

commit v6 on v5

--- a/solution.py
+++ b/solution.py
@@ -279,17 +279,22 @@
 
     for load in loads[7:]:
         load.start()
-    for load in loads[:7]:
+    for load in loads[:3]:
         load.start()
+    loads[7].wait()
+    loads[8].wait()
     pl.semaphore_wait(bar, PLANE + planes - 1 + far.astype(jnp.int32))
 
-    c_frames = remote(frames_hbm, fb.at[hy], 0, partner)
+    c_decay = [remote(db.at[q], db.at[q], S_DECAY + k, peer) for k, peer in enumerate(peers)]
+    for c in c_decay:
+        c.start()
+    c_frames = remote(fb.at[hy], fb.at[hy], 0, partner)
     c_frames.start()
     step = rows // CHUNKS
 
     def off_copy(i):
         part = pl.ds(i * step, step)
-        return remote(frames_hbm.at[part, :], ob.at[hy, part, :], S_OFF + i, off)
+        return remote(fb.at[hy, part, :], ob.at[hy, part, :], S_OFF + i, off)
 
     def on_copy(i):
         part = pl.ds(i * step, step)
@@ -306,11 +311,7 @@
         for i in range(CHUNKS):
             off_copy(i).start()
 
-    c_decay = [remote(decay_hbm, db.at[q], S_DECAY + k, peer) for k, peer in enumerate(peers)]
-    for c in c_decay:
-        c.start()
-
-    for load in loads[7:]:
+    for load in loads[9:]:
         load.wait()
 
     def id_row(at):
@@ -392,6 +393,8 @@
         c_t.start()
 
     c_frames.wait()
+    for load in loads[3:7]:
+        load.start()
     normalize(fb)
 
     def project(which, dst, scale):
@@ -401,7 +404,7 @@
             dst[:, cols] = part * scale if scale is not None else part
             return carry
 
-        lax.fori_loop(0, width // 256, tile, 0)
+        lax.fori_loop(0, width // 256, tile, 0, unroll=True)
 
     loads[0].wait()
     project(1, kb.at[0], None)
@@ -525,13 +528,13 @@
         return carry
 
     tiles = wx.shape[1] // 256
-    lax.fori_loop(0, tiles // 2 + 1, drive_in, 0)
+    lax.fori_loop(0, tiles // 2 + 1, drive_in, 0, unroll=True)
     c_cp.wait()
     c_bc = [remote(cp, bcb.at[:, q], S_BC + k - 1, peers[k - 1]) for k in range(1, PLANE)]
     for c in c_bc:
         c.start()
     bcb[:, q] = cp[...]
-    lax.fori_loop(tiles // 2 + 1, tiles, drive_in, 0)
+    lax.fori_loop(tiles // 2 + 1, tiles, drive_in, 0, unroll=True)
     for j in range(PLANE):
         xq[j] = xin[:, j * qw : (j + 1) * qw].astype(BF16)
     c_x = [remote(xq.at[(q + k) % PLANE], xb.at[q], S_X + k - 1, peers[k - 1]) for k in range(1, PLANE)]

time: 66.8 us -> 62.8 us (0.940); the launches traced: 66.7 us -> 61.8 us
  Pallas kernels: 66 us -> 61.2 us
    pallas_call x1, Pallas kernels: 64.2 us -> 59.4 us  [per_device(): pl.pallas_call(functools.partial(fused_kernel, nt), out_shape=(jax.ShapeD...]
where the time goes in v6:
time: 62.8 us; the launch traced here: 61.8 us
  Pallas kernels  61.2 us (97%)
  between operations  0.64 us (1%)
    pallas_call x1, Pallas kernels, per_device(): pl.pallas_call(functools.partial(fused_kernel, nt), out_shape=(jax.ShapeD...  59.4 us
    pallas_call x1, Pallas kernels, per_device(): pl.pallas_call(place_kernel, out_shape=(jax.ShapeDtypeStruct(encoded.shap...  1.82 us

profile of v6, /device:TPU:27, one launch (start us, length us, event | category | flops | bytes accessed | tf_op | source)
XLA Modules:
  0.0 61.8 jit_solution(9183609817036969204)
XLA Ops:
  0.6 59.4 %shard_map.140 = (bf16[256,640]{1,0:T(8,128)(2,1)}, bf16[64,1280]{1,0:T(8,128)(2,1)}) custom-call(bf16[256,640]{1,0:T(8,128)(2,1)} %frames_hbm.1, s32[4096]{0:T(1024)} %ids_hbm.1, f32[1280]{0:T(1024)} %lng_hbm.1, f32[1280]{0:T(1024)} %lnb_hbm.1, bf16[3,1280,512]{2,1,0:T(8,128)(2,1)} %qkv_hbm.1, bf16[1024,640]{1,0:T(8,128)(2,1)} %out_hbm.1, f32[640]{0:T(1024)} %ob_hbm.1, ...), custom_call_target="tpu_custom_call" | custom-call | tf_op jit(solution)/shard_map/pallas_call | solution.py:636
  60.0 1.8 %shard_map.141 = (bf16[256,640]{1,0:T(8,128)(2,1)}, bf16[64,1280]{1,0:T(8,128)(2,1)}) custom-call(bf16[256,640]{1,0:T(8,128)(2,1)} %get-tuple-element.4.a, bf16[64,1280]{1,0:T(8,128)(2,1)} %get-tuple-element.5.b), custom_call_target="tpu_custom_call" | custom-call | tf_op jit(solution)/shard_map/pallas_call | solution.py:700

commit v7 on v6

--- a/solution.py
+++ b/solution.py
@@ -421,6 +421,10 @@
 
     sides = (jnp.where(is_low, 1.0, 0.0).astype(BF16), jnp.where(is_low, 0.0, 1.0).astype(BF16))
 
+    def row_sums(got):
+        crossed = jnp.where(is_low, got[1][0], got[0][0])
+        return jnp.concatenate([crossed[:, EHEAD_DIM:], crossed[:, :EHEAD_DIM]], axis=1)
+
     def within_chip(p, carry):
         cols = pl.ds(pl.multiple_of(p * 128, 128), 128)
         qp = qb[:, cols]
@@ -431,15 +435,15 @@
             s = dot(qp * side, kp, NT) + mk[:, : 2 * rows]
             m = jnp.max(s, axis=-1, keepdims=True)
             e = jnp.exp(s - m)
-            got.append((dot(e.astype(BF16), vp), m, jnp.sum(e, axis=-1, keepdims=True)))
+            got.append((dot(e.astype(BF16), vp * side + (1 - side)), m))
         acc[p] = jnp.where(is_low, got[0][0], got[1][0])
         mb[p] = jnp.where(is_low, got[0][1], got[1][1])
-        lb[p] = jnp.where(is_low, got[0][2], got[1][2])
+        lb[p] = row_sums(got)
         return carry
 
     c_k.wait()
     c_v.wait()
-    lax.fori_loop(0, pairs, within_chip, 0)
+    lax.fori_loop(0, pairs, within_chip, 0, unroll=2)
 
     @pl.when(has_off)
     def _():
@@ -470,15 +474,15 @@
             m1 = old_m[:, i * EHEAD_DIM : i * EHEAD_DIM + 1]
             m = jnp.maximum(jnp.max(s, axis=-1, keepdims=True), m1)
             e = jnp.exp(s - m)
-            got.append((dot(e.astype(BF16), vp), m, jnp.sum(e, axis=-1, keepdims=True)))
+            got.append((dot(e.astype(BF16), vp * side + (1 - side)), m))
         fade = jnp.exp(old_m - jnp.where(is_low, got[0][1], got[1][1]))
-        total = old_l * fade + jnp.where(is_low, got[0][2], got[1][2])
+        total = old_l * fade + row_sums(got)
         blended = acc[p] * fade + jnp.where(is_low, got[0][0], got[1][0])
         att[:, pl.ds(pl.multiple_of(hy * width + p * 128, 128), 128)] = (blended / total).astype(BF16)
         att_copy(p).start()
         return carry
 
-    lax.fori_loop(0, pairs, beyond_chip, 0)
+    lax.fori_loop(0, pairs, beyond_chip, 0, unroll=2)
     for p in range(pairs):
         att_copy(p).wait()
 

time: 62.8 us -> 62.8 us (level)
  no operation moved by 1% of the time
where the time goes in v7:
time: 62.8 us; the launch traced here: 61.9 us
  Pallas kernels  61.3 us (98%)
  between operations  0.64 us (1%)
    pallas_call x1, Pallas kernels, per_device(): pl.pallas_call(functools.partial(fused_kernel, nt), out_shape=(jax.ShapeD...  59.4 us
    pallas_call x1, Pallas kernels, per_device(): pl.pallas_call(place_kernel, out_shape=(jax.ShapeDtypeStruct(encoded.shap...  1.82 us

profile of v7, /device:TPU:27, one launch (start us, length us, event | category | flops | bytes accessed | tf_op | source)
XLA Modules:
  0.0 61.9 jit_solution(2105481698456776588)
XLA Ops:
  0.6 59.4 %shard_map.140 = (bf16[256,640]{1,0:T(8,128)(2,1)}, bf16[64,1280]{1,0:T(8,128)(2,1)}) custom-call(bf16[256,640]{1,0:T(8,128)(2,1)} %frames_hbm.1, s32[4096]{0:T(1024)} %ids_hbm.1, f32[1280]{0:T(1024)} %lng_hbm.1, f32[1280]{0:T(1024)} %lnb_hbm.1, bf16[3,1280,512]{2,1,0:T(8,128)(2,1)} %qkv_hbm.1, bf16[1024,640]{1,0:T(8,128)(2,1)} %out_hbm.1, f32[640]{0:T(1024)} %ob_hbm.1, ...), custom_call_target="tpu_custom_call" | custom-call | tf_op jit(solution)/shard_map/pallas_call | solution.py:640
  60.1 1.8 %shard_map.141 = (bf16[256,640]{1,0:T(8,128)(2,1)}, bf16[64,1280]{1,0:T(8,128)(2,1)}) custom-call(bf16[256,640]{1,0:T(8,128)(2,1)} %get-tuple-element.4.a, bf16[64,1280]{1,0:T(8,128)(2,1)} %get-tuple-element.5.b), custom_call_target="tpu_custom_call" | custom-call | tf_op jit(solution)/shard_map/pallas_call | solution.py:704
